TPU v7x, 256 devices: a whole 4x4x8 slice. The times are simulated.
256 devices in a mesh: seq: 128 (over y, z, x), pipe: 2 (over core).
Axes of the slice: x: 4, y: 4, z: 8, core: 2. Of those that a mesh axis runs over, the one named last changes fastest.
Arguments:
- query_key: bfloat16 [2, 16384, 2048], P('pipe', 'seq'), may hold values from -6 to 6
- payload_matrix: bfloat16 [2, 16384, 2048], P('pipe', 'seq'), may hold values from -6 to 6
- out_grad: bfloat16 [2, 16384, 2048], P('pipe', 'seq'), may hold values from -6 to 6
- route_assignment: int32 [2, 128, 16], P('pipe'), may hold values from 0 to 63, as said below
Outputs:
- attn_out: bfloat16 [2, 16384, 2048], P('pipe', 'seq')
- grad_qk: bfloat16 [2, 16384, 2048], P('pipe', 'seq')
- grad_v: bfloat16 [2, 16384, 2048], P('pipe', 'seq')
Inputs may be any that keep to these rules, and one draw needn't show every extreme that they name: `route_assignment`: in each section and head every cluster holds exactly 2 tiles. Cluster c of head h is owned by device 2 * c + (h mod 2) of seq. The 16 tile-head pairs of the tiles of one index of seq fall into clusters owned by one device at most 1 times, and exactly 1 times for some owner.
All inputs are finite; a program needn't handle non-finite values.
Results may differ from a plain program's by a relative error of at most 0.012.
The roundings to bfloat16 on the way count: a program that leaves them out, or rounds other values in their place, can miss the bound.
Values may be sent and summed in bfloat16 or wider, within the bound.
No kernel may reach another device: no remote copies, remote signals or barrier semaphores. Data moves between devices by JAX's collectives and lax.ppermute only.
A program may use at most 128 MiB of HBM per device.

v0:
```python
import jax
import jax.numpy as jnp
from jax import lax
from jax.sharding import PartitionSpec as P

HEADS = 16
HEAD_DIM = 128
TILE = 128
TILES_DEV = 1
MOST = 2


logit_divisor_heat = 4.0
epsilon = 1e-06


def shifted(value, axis, by):
    count = lax.axis_size(axis)
    return lax.ppermute(value, axis, [(i, (i + by) % count) for i in range(count)])


def cluster_members(cluster_labels, cluster, most_tiles):
    hit_mask = cluster_labels == cluster
    rank_pos = jnp.cumsum(hit_mask.astype(jnp.int32)) - 1
    target = jnp.where(hit_mask, rank_pos, most_tiles)
    tile_ids = jnp.arange(cluster_labels.shape[0], dtype=jnp.int32)
    member_ids = jnp.zeros((most_tiles,), jnp.int32).at[target].set(tile_ids, mode="drop")
    member_count = jnp.sum(hit_mask.astype(jnp.int32))
    return (member_ids, jnp.arange(most_tiles, dtype=jnp.int32) < member_count)


def cluster_forward(common_lookup_vectors, values_in, positions, valid_rows):
    logit_multiplier = logit_divisor_heat / common_lookup_vectors.shape[-1]
    scores = (
        jnp.dot(common_lookup_vectors, common_lookup_vectors.T, preferred_element_type=jnp.float32)
        * logit_multiplier
    )
    allowed = valid_rows[None, :] & (positions[None, :] <= positions[:, None]) | jnp.eye(
        positions.shape[0], dtype=bool
    )
    weights = jnp.where(allowed, jnp.exp(scores), jnp.zeros_like(scores))
    attn_probs = (weights / jnp.sum(weights, axis=1, keepdims=True)).astype(jnp.bfloat16)
    output = jnp.dot(attn_probs, values_in, preferred_element_type=jnp.float32).astype(jnp.bfloat16)
    return (output, attn_probs)


def cluster_backward(common_lookup_vectors, values_in, attn_probs, grad_rows, valid_rows):
    logit_multiplier = logit_divisor_heat / common_lookup_vectors.shape[-1]
    grad_rows = jnp.where(valid_rows[:, None], grad_rows, jnp.zeros_like(grad_rows))
    grad_probs = jnp.dot(grad_rows, values_in.T, preferred_element_type=jnp.float32)
    prob_values = attn_probs.astype(jnp.float32)
    row_total = jnp.sum(prob_values * grad_probs, axis=1, keepdims=True)
    grad_scores = (prob_values * (grad_probs - row_total) * logit_multiplier).astype(jnp.bfloat16)
    grad_query = jnp.dot(grad_scores, common_lookup_vectors, preferred_element_type=jnp.float32)
    grad_query = grad_query + jnp.dot(
        grad_scores.T, common_lookup_vectors, preferred_element_type=jnp.float32
    )
    sensitivity_of_outputs = jnp.dot(attn_probs.T, grad_rows, preferred_element_type=jnp.float32)
    return (grad_query.astype(jnp.bfloat16), sensitivity_of_outputs.astype(jnp.bfloat16))


def split_items(row_block, tiles_here, head_count, tile_len, head_width):
    shaped = row_block.reshape(tiles_here, tile_len, head_count, head_width)
    return jnp.transpose(shaped, (0, 2, 1, 3)).reshape(
        tiles_here * head_count, tile_len, head_width
    )


def join_items(item_block, tiles_here, head_count, tile_len, head_width):
    shaped = item_block.reshape(tiles_here, head_count, tile_len, head_width)
    return jnp.transpose(shaped, (0, 2, 1, 3)).reshape(
        tiles_here * tile_len, head_count * head_width
    )


def local(query_key, payload_matrix, out_grad, route_assignment):
    batch_length_total = lax.axis_size("seq")
    self_index = lax.axis_index("seq")
    tile_len = TILE
    head_width = HEAD_DIM
    head_count = HEADS
    tiles_here = TILES_DEV
    most_tiles = MOST
    half_heads = head_count // 2
    cluster_total = batch_length_total // 2
    cap_slots = max(1, head_count * tiles_here // batch_length_total)
    slot_total = batch_length_total * cap_slots
    item_count = tiles_here * head_count
    cluster_labels = route_assignment[0]
    reader_roster = jnp.arange(head_count, dtype=jnp.int32)
    cluster_grid = jnp.arange(cluster_total, dtype=jnp.int32)
    keeper_register = 2 * cluster_grid[None, :] + (reader_roster % 2)[:, None]
    dest_all = keeper_register[reader_roster[None, :], cluster_labels]
    item_grid = jnp.arange(item_count, dtype=jnp.int32)
    earlier = item_grid[None, :] < item_grid[:, None]
    same_dest = dest_all[:, :, None] == dest_all[:, None, :]
    rank_all = jnp.sum((same_dest & earlier[None, :, :]).astype(jnp.int32), axis=2)
    own_dest = lax.dynamic_index_in_dim(dest_all, self_index, 0, keepdims=False)
    own_rank = lax.dynamic_index_in_dim(rank_all, self_index, 0, keepdims=False)
    send_rows = own_dest * cap_slots + own_rank
    raw_qk = query_key[0].astype(jnp.float32).reshape(-1, head_count, head_width)
    factor = lax.rsqrt(jnp.mean(raw_qk * raw_qk, axis=-1, keepdims=True) + epsilon)
    normed = (raw_qk * factor).astype(jnp.bfloat16).reshape(-1, head_count * head_width)

    def pack_send(row_block):
        item_block = split_items(row_block, tiles_here, head_count, tile_len, head_width)
        empty = jnp.zeros((slot_total, tile_len, head_width), row_block.dtype)
        return empty.at[send_rows].set(item_block)

    def unpack_back(received):
        return join_items(received[send_rows], tiles_here, head_count, tile_len, head_width)

    parity = self_index % 2
    owned_heads = 2 * jnp.arange(half_heads, dtype=jnp.int32) + parity
    owned_ids = jnp.full((half_heads,), self_index // 2, dtype=jnp.int32)

    def members_of(head_id, cluster):
        head_labels = lax.dynamic_index_in_dim(cluster_labels, head_id, 1, keepdims=False)
        return cluster_members(head_labels, cluster, most_tiles)

    member_ids, member_valid = jax.vmap(members_of)(owned_heads, owned_ids)
    member_source = member_ids // tiles_here
    member_item = member_ids % tiles_here * head_count + owned_heads[:, None]
    member_slot = member_source * cap_slots + rank_all[member_source, member_item]
    gather_slot = member_slot.reshape(-1)
    drop_slot = jnp.where(member_valid, member_slot, slot_total).reshape(-1)
    tile_offsets = jnp.arange(tile_len, dtype=jnp.int32)
    positions = (member_ids[:, :, None] * tile_len + tile_offsets[None, None, :]).reshape(
        half_heads, -1
    )
    valid_rows = jnp.repeat(member_valid, tile_len, axis=1)

    def gather_groups(received):
        return received[gather_slot].reshape(half_heads, most_tiles * tile_len, head_width)

    def distribute_buckets(grouped):
        flat_items = grouped.reshape(-1, tile_len, head_width)
        empty = jnp.zeros((slot_total, tile_len, head_width), grouped.dtype)
        return empty.at[drop_slot].set(flat_items, mode="drop")

    qk_items = pack_send(normed)
    value_items = pack_send(payload_matrix[0])
    grad_items = pack_send(out_grad[0])
    got_qk, got_values = (
        lax.all_to_all(qk_items, "seq", split_axis=0, concat_axis=0, tiled=True),
        lax.all_to_all(value_items, "seq", split_axis=0, concat_axis=0, tiled=True),
    )
    group_qk = gather_groups(got_qk)
    group_values = gather_groups(got_values)

    def forward_one_group(input_arrays):
        return cluster_forward(input_arrays[0], input_arrays[1], input_arrays[2], input_arrays[3])

    group_out, group_probs = lax.map(
        forward_one_group, (group_qk, group_values, positions, valid_rows)
    )
    back_out = lax.all_to_all(
        distribute_buckets(group_out), "seq", split_axis=0, concat_axis=0, tiled=True
    )
    got_grad = lax.all_to_all(grad_items, "seq", split_axis=0, concat_axis=0, tiled=True)

    def backward_one_group(input_arrays):
        return cluster_backward(
            input_arrays[0], input_arrays[1], input_arrays[2], input_arrays[3], input_arrays[4]
        )

    group_query_key_gradient, group_dv = lax.map(
        backward_one_group,
        (group_qk, group_values, group_probs, gather_groups(got_grad), valid_rows),
    )
    back_dqk, back_dv = (
        lax.all_to_all(
            distribute_buckets(group_query_key_gradient),
            "seq",
            split_axis=0,
            concat_axis=0,
            tiled=True,
        ),
        lax.all_to_all(
            distribute_buckets(group_dv), "seq", split_axis=0, concat_axis=0, tiled=True
        ),
    )
    attention = unpack_back(back_out)
    grad_normed = unpack_back(back_dqk).astype(jnp.float32).reshape(-1, head_count, head_width)
    grad_raw = factor * grad_normed - raw_qk * factor**3 * jnp.mean(
        raw_qk * grad_normed, axis=-1, keepdims=True
    )
    grad_input = grad_raw.reshape(-1, head_count * head_width).astype(jnp.bfloat16)
    grad_value = unpack_back(back_dv)
    passed_qk, passed_values = shifted((grad_input, grad_value), "pipe", -1)
    return (attention[None], passed_qk[None], passed_values[None])


def solution(mesh):
    placed = (
        P("pipe", "seq", None),
        P("pipe", "seq", None),
        P("pipe", "seq", None),
        P("pipe", None, None),
    )
    return jax.shard_map(
        local,
        mesh=mesh,
        in_specs=placed,
        out_specs=(P("pipe", "seq", None), P("pipe", "seq", None), P("pipe", "seq", None)),
        check_vma=False,
    )
```

profile of v0, /device:TPU:1, one launch (start us, length us, event | category | flops | bytes accessed | tf_op | source)
XLA Modules:
  0.0 742.2 jit_solution(2750241487457169096)
XLA Ops:
  0.7 1.3 gather_fusion
  3.5 23.6 %compare_select_fusion = s32[8,128,1]{2,0,1:T(8,128)S(1)} fusion(pred[8,128,1]{2,0,1:T(8,128)(4,1)S(1)} %copy.113, s32[8,128,1]{2,0,1:T(8,128)S(1)} %copy.112), kind=kOutput, calls=%fused_computation.66 | output fusion | flops 135168 | bytes 9216 | tf_op jit(solution)/shard_map/vmap(jit(cumsum))/reduce_window_sum | solution.py:24
  29.1 4.3 scatter_custom_fusion.6
  34.0 13.6 %gather_fusion.1 = s32[2048]{0:T(1024)S(1)} fusion(s32[16,64]{1,0:T(8,128)S(1)} %broadcast_add_fusion, s32[2048]{0:T(1024)S(1)} %reshape.405), kind=kCustom, calls=%fused_computation.1 | custom fusion | bytes 32768 | tf_op jit(solution)/shard_map/gather | solution.py:93
  49.2 3.0 broadcast.349.clone.2
  52.2 2.6 scatter_fusion.1
  54.8 17.0 %all-to-all-start.1 = ((bf16[128,128,128]{2,1,0:T(8,128)(2,1)}), bf16[128,128,128]{2,1,0:T(8,128)(2,1)}, u32[]{:S(2)}, u32[]{:S(2)}) async-start(bf16[128,128,128]{2,1,0:T(8,128)(2,1)} %scatter_fusion.1), calls=%async_computation.1 | async-start | bytes 8388608 | tf_op jit(solution)/shard_map/all_to_all | solution.py:146
  73.0 3.0 broadcast.349.clone.1
  75.9 2.6 scatter_fusion
  78.5 86.1 %all-to-all-done.1 = bf16[128,128,128]{2,1,0:T(8,128)(2,1)} async-done(((bf16[128,128,128]{2,1,0:T(8,128)(2,1)}), bf16[128,128,128]{2,1,0:T(8,128)(2,1)}, u32[]{:S(2)}, u32[]{:S(2)}) %all-to-all-start.1) | async-done | bytes 4194336 | tf_op jit(solution)/shard_map/all_to_all | solution.py:146
  164.6 11.1 %all-to-all-start = ((bf16[128,128,128]{2,1,0:T(8,128)(2,1)}), bf16[128,128,128]{2,1,0:T(8,128)(2,1)}, u32[]{:S(2)}, u32[]{:S(2)}) async-start(bf16[128,128,128]{2,1,0:T(8,128)(2,1)} %scatter_fusion), calls=%async_computation | async-start | bytes 8388608 | tf_op jit(solution)/shard_map/all_to_all | solution.py:145
  175.9 3.0 broadcast.349.clone.4
  178.9 2.6 scatter_fusion.3
  181.5 86.8 %all-to-all-done = bf16[128,128,128]{2,1,0:T(8,128)(2,1)} async-done(((bf16[128,128,128]{2,1,0:T(8,128)(2,1)}), bf16[128,128,128]{2,1,0:T(8,128)(2,1)}, u32[]{:S(2)}, u32[]{:S(2)}) %all-to-all-start) | async-done | bytes 4194336 | tf_op jit(solution)/shard_map/all_to_all | solution.py:145
  268.3 11.2 %all-to-all-start.3 = ((bf16[128,128,128]{2,1,0:T(8,128)(2,1)}), bf16[128,128,128]{2,1,0:T(8,128)(2,1)}, u32[]{:S(2)}, u32[]{:S(2)}) async-start(bf16[128,128,128]{2,1,0:T(8,128)(2,1)} %scatter_fusion.3), calls=%async_computation.3 | async-start | bytes 8388608 | tf_op jit(solution)/shard_map/all_to_all | solution.py:160
  279.9 3.6 gather_fusion.4
  283.5 2.8 gather_fusion.3
  286.4 16.5 %while.24 = (s32[]{:T(128)}, bf16[8,256,128]{2,1,0:T(8,128)(2,1)S(1)}, bf16[8,256,256]{1,2,0:T(8,128)(2,1)}, pred[8,256]{1,0:T(8,128)(4,1)S(1)}, s32[8,256]{1,0:...) while((s32[]{:T(128)}, bf16[8,256,128]{2,1,0:T(8,128)(2,1)S(1)}, ...), condition=%wide.region_9.10_spmd, body=%wide.region_7.9_spmd.sunk | while | flops 34307840 | bytes 1123937 | solution.py:154
  302.9 69.1 %all-to-all-done.3 = bf16[128,128,128]{2,1,0:T(8,128)(2,1)} async-done(((bf16[128,128,128]{2,1,0:T(8,128)(2,1)}), bf16[128,128,128]{2,1,0:T(8,128)(2,1)}, u32[]{:S(2)}, u32[]{:S(2)}) %all-to-all-start.3) | async-done | bytes 4194336 | tf_op jit(solution)/shard_map/all_to_all | solution.py:160
  372.1 3.6 gather_fusion.6
  377.4 40.7 %while.25 = (s32[]{:T(128)}, bf16[8,256,128]{2,1,0:T(8,128)(2,1)}, bf16[8,256,128]{2,1,0:T(8,128)(2,1)}, bf16[8,256,256]{1,2,0:T(8,128)(2,1)}, pred[8,256]{1,0:T...) while((s32[]{:T(128)}, bf16[8,256,128]{2,1,0:T(8,128)(2,1)}, ...), condition=%wide.region_14.15_spmd, body=%wide.region_12.14_spmd.sunk | while | flops 67796736 | bytes 2038889 | solution.py:167
  380.7 1.8 fusion.90
  385.8 1.8 fusion.90
  390.8 1.8 fusion.90
  392.7 1.3 fusion.86
  395.9 1.8 fusion.90
  401.0 1.8 fusion.90
  402.9 1.3 fusion.86
  406.1 1.8 fusion.90
  411.2 1.8 fusion.90
  416.3 1.8 fusion.90
  418.1 3.0 broadcast.349.clone.5
  421.1 2.6 scatter_fusion.5
  423.7 11.2 %all-to-all-start.5 = ((bf16[128,128,128]{2,1,0:T(8,128)(2,1)}), bf16[128,128,128]{2,1,0:T(8,128)(2,1)}, u32[]{:S(2)}, u32[]{:S(2)}) async-start(bf16[128,128,128]{2,1,0:T(8,128)(2,1)} %scatter_fusion.5), calls=%async_computation.5 | async-start | bytes 8388608 | tf_op jit(solution)/shard_map/all_to_all | solution.py:179
  434.9 3.0 broadcast.349.clone.3
  438.0 2.6 scatter_fusion.4
  440.5 86.8 %all-to-all-done.5 = bf16[128,128,128]{2,1,0:T(8,128)(2,1)} async-done(((bf16[128,128,128]{2,1,0:T(8,128)(2,1)}), bf16[128,128,128]{2,1,0:T(8,128)(2,1)}, u32[]{:S(2)}, u32[]{:S(2)}) %all-to-all-start.5) | async-done | bytes 4194336 | tf_op jit(solution)/shard_map/all_to_all | solution.py:179
  527.3 11.4 %all-to-all-start.4 = ((bf16[128,128,128]{2,1,0:T(8,128)(2,1)}), bf16[128,128,128]{2,1,0:T(8,128)(2,1)}, u32[]{:S(2)}, u32[]{:S(2)}) async-start(bf16[128,128,128]{2,1,0:T(8,128)(2,1)} %scatter_fusion.4), calls=%async_computation.4 | async-start | bytes 8388608 | tf_op jit(solution)/shard_map/all_to_all | solution.py:172
  538.7 3.0 broadcast.349.clone
  541.7 2.6 scatter_fusion.2
  544.3 87.0 %all-to-all-done.4 = bf16[128,128,128]{2,1,0:T(8,128)(2,1)} async-done(((bf16[128,128,128]{2,1,0:T(8,128)(2,1)}), bf16[128,128,128]{2,1,0:T(8,128)(2,1)}, u32[]{:S(2)}, u32[]{:S(2)}) %all-to-all-start.4) | async-done | bytes 4194336 | tf_op jit(solution)/shard_map/all_to_all | solution.py:172
  631.3 11.4 %all-to-all-start.2 = ((bf16[128,128,128]{2,1,0:T(8,128)(2,1)}), bf16[128,128,128]{2,1,0:T(8,128)(2,1)}, u32[]{:S(2)}, u32[]{:S(2)}) async-start(bf16[128,128,128]{2,1,0:T(8,128)(2,1)} %scatter_fusion.2), calls=%async_computation.2 | async-start | bytes 8388608 | tf_op jit(solution)/shard_map/all_to_all | solution.py:157
  643.1 2.8 gather_fusion.8
  646.9 1.9 collective-permute-start.1
  648.8 2.8 gather_fusion.7
  652.8 82.2 %all-to-all-done.2 = bf16[128,128,128]{2,1,0:T(8,128)(2,1)} async-done(((bf16[128,128,128]{2,1,0:T(8,128)(2,1)}), bf16[128,128,128]{2,1,0:T(8,128)(2,1)}, u32[]{:S(2)}, u32[]{:S(2)}) %all-to-all-start.2) | async-done | bytes 4194336 | tf_op jit(solution)/shard_map/all_to_all | solution.py:157
  735.0 2.8 gather_fusion.5
  739.1 2.0 copy.136
  (163 shorter events, 53.6 us)
Async XLA Ops:
  0.6 48.4 %copy-start = (bf16[1,128,2048]{2,1,0:T(8,128)(2,1)S(1)}, bf16[1,128,2048]{2,1,0:T(8,128)(2,1)}, u32[]{:S(2)}) copy-start(bf16[1,128,2048]{2,1,0:T(8,128)(2,1)} %param.9) | copy-start | bytes 1572868
  54.8 17.0 %copy-start.4 = (bf16[1,128,2048]{2,1,0:T(8,128)(2,1)S(1)}, bf16[1,128,2048]{2,1,0:T(8,128)(2,1)}, u32[]{:S(2)}) copy-start(bf16[1,128,2048]{2,1,0:T(8,128)(2,1)} %param.8) | copy-start | bytes 1572868
  54.8 109.8 %all-to-all-start.1 = ((bf16[128,128,128]{2,1,0:T(8,128)(2,1)}), bf16[128,128,128]{2,1,0:T(8,128)(2,1)}, u32[]{:S(2)}, u32[]{:S(2)}) async-start(bf16[128,128,128]{2,1,0:T(8,128)(2,1)} %scatter_fusion.1), calls=%async_computation.1 | async-start | bytes 8388608 | tf_op jit(solution)/shard_map/all_to_all | solution.py:146
  78.5 97.2 %copy-start.5 = (bf16[1,128,2048]{2,1,0:T(8,128)(2,1)S(1)}, bf16[1,128,2048]{2,1,0:T(8,128)(2,1)}, u32[]{:S(2)}) copy-start(bf16[1,128,2048]{2,1,0:T(8,128)(2,1)} %param.10) | copy-start | bytes 1572868
  164.6 103.7 %all-to-all-start = ((bf16[128,128,128]{2,1,0:T(8,128)(2,1)}), bf16[128,128,128]{2,1,0:T(8,128)(2,1)}, u32[]{:S(2)}, u32[]{:S(2)}) async-start(bf16[128,128,128]{2,1,0:T(8,128)(2,1)} %scatter_fusion), calls=%async_computation | async-start | bytes 8388608 | tf_op jit(solution)/shard_map/all_to_all | solution.py:145
  268.3 103.8 %all-to-all-start.3 = ((bf16[128,128,128]{2,1,0:T(8,128)(2,1)}), bf16[128,128,128]{2,1,0:T(8,128)(2,1)}, u32[]{:S(2)}, u32[]{:S(2)}) async-start(bf16[128,128,128]{2,1,0:T(8,128)(2,1)} %scatter_fusion.3), calls=%async_computation.3 | async-start | bytes 8388608 | tf_op jit(solution)/shard_map/all_to_all | solution.py:160
  418.1 3.0 copy-start.3
  423.7 103.6 %all-to-all-start.5 = ((bf16[128,128,128]{2,1,0:T(8,128)(2,1)}), bf16[128,128,128]{2,1,0:T(8,128)(2,1)}, u32[]{:S(2)}, u32[]{:S(2)}) async-start(bf16[128,128,128]{2,1,0:T(8,128)(2,1)} %scatter_fusion.5), calls=%async_computation.5 | async-start | bytes 8388608 | tf_op jit(solution)/shard_map/all_to_all | solution.py:179
  434.9 3.0 copy-start.2
  527.3 103.9 %all-to-all-start.4 = ((bf16[128,128,128]{2,1,0:T(8,128)(2,1)}), bf16[128,128,128]{2,1,0:T(8,128)(2,1)}, u32[]{:S(2)}, u32[]{:S(2)}) async-start(bf16[128,128,128]{2,1,0:T(8,128)(2,1)} %scatter_fusion.4), calls=%async_computation.4 | async-start | bytes 8388608 | tf_op jit(solution)/shard_map/all_to_all | solution.py:172
  631.3 103.7 %all-to-all-start.2 = ((bf16[128,128,128]{2,1,0:T(8,128)(2,1)}), bf16[128,128,128]{2,1,0:T(8,128)(2,1)}, u32[]{:S(2)}, u32[]{:S(2)}) async-start(bf16[128,128,128]{2,1,0:T(8,128)(2,1)} %scatter_fusion.2), calls=%async_computation.2 | async-start | bytes 8388608 | tf_op jit(solution)/shard_map/all_to_all | solution.py:157
  646.9 92.2 %collective-permute-start.1 = (bf16[128,2048]{0,1:T(8,128)(2,1)}, bf16[128,2048]{0,1:T(8,128)(2,1)}, u32[]{:S(2)}, u32[]{:S(2)}) collective-permute-start(bf16[128,2048]{0,1:T(8,128)(2,1)} %bitcast.54), channel_id=1, source_target_pairs={{0,1},{1,0},{2,3},{3,2},{4,5},{5,4},{6,7},{7,6},{8,9},{9,8},{10,11... | collective-permute-start | bytes 1572872 | tf_op jit(solution)/shard_map/ppermute | solution.py:19
  652.1 90.1 %copy-start.1 = (bf16[1,128,2048]{2,1,0:T(8,128)(2,1)S(1)}, bf16[1,128,2048]{2,1,0:T(8,128)(2,1)}, u32[]{:S(2)}) copy-start(bf16[1,128,2048]{2,1,0:T(8,128)(2,1)} %param.9) | copy-start | bytes 1572868
  652.7 88.5 %collective-permute-start = (bf16[128,2048]{0,1:T(8,128)(2,1)S(1)}, bf16[128,2048]{0,1:T(8,128)(2,1)S(1)}, u32[]{:S(2)}, u32[]{:S(2)}) collective-permute-start(bf16[128,2048]{0,1:T(8,128)(2,1)S(1)} %fusion.40), channel_id=1, source_target_pairs={{0,1},{1,0},{2,3},{3,2},{4,5},{5,4},{6,7},{7,6},{8,9},{9,8},{10,11... | collective-permute-start | bytes 1572872 | tf_op jit(solution)/shard_map/ppermute | solution.py:19
where the time goes:
time: 748 us; the launch traced here: 742 us
  waiting for transfers between devices  498 us (67%)
  local copies, waits for them, and re-layouts  83.3 us (11%)
  starting transfers between devices  75.4 us (10%)
  matrix products  43.4 us (6%)
  other arithmetic  40.7 us (5%)
    all_to_all x1, waiting for transfers between devices, local(): lax.all_to_all(distribute_buckets(group_query_key_gradient), 'seq', split...  87 us
    all_to_all x1, waiting for transfers between devices, local(): lax.all_to_all(qk_items, 'seq', split_axis=0, concat_axis=0, tiled=True)  86.8 us
    all_to_all x1, waiting for transfers between devices, local(): lax.all_to_all(distribute_buckets(group_dv), 'seq', split_axis=0, concat_...  86.8 us
    all_to_all x1, waiting for transfers between devices, local(): lax.all_to_all(value_items, 'seq', split_axis=0, concat_axis=0, tiled=True)  86.1 us
    all_to_all x1, waiting for transfers between devices, local(): lax.all_to_all(distribute_buckets(group_out), 'seq', split_axis=0, concat...  82.2 us
    all_to_all x1, waiting for transfers between devices, local(): lax.all_to_all(grad_items, 'seq', split_axis=0, concat_axis=0, tiled=True)  69.1 us
    another operation x1, other arithmetic, cluster_members(): rank_pos = jnp.cumsum(hit_mask.astype(jnp.int32)) - 1  23.6 us
    another operation x9, local copies, waits for them, and re-layouts  19.8 us
  transfers between devices with their start and end apart: 8, of which 6 were waited for; matrix products, arithmetic and copies ran while one was open for 8% of the time, Pallas kernels for 0%

commit v1 on v0

v1 whole, which is shorter than its diff:
```python
import jax
import jax.numpy as jnp
from jax import lax
from jax.experimental import pallas as pl
from jax.experimental.pallas import tpu as pltpu
from jax.sharding import PartitionSpec as P

HEADS = 16
HEAD_DIM = 128
TILE = 128
TILES = 128
SLICES = 8
ROWS = TILE // SLICES
MSG = 2 * ROWS + 8
STEP_HEADS = 4
STEPS = HEADS // STEP_HEADS
STEP_COLS = STEP_HEADS * HEAD_DIM
EPSILON = 1e-06
SCALE = 4.0 / HEAD_DIM
F32 = jnp.float32
BF16 = jnp.bfloat16


def dot_nt(a, b):
    return lax.dot_general(a, b, (((1,), (1,)), ((), ())), preferred_element_type=F32)


def dot_nn(a, b):
    return lax.dot_general(a, b, (((1,), (0,)), ((), ())), preferred_element_type=F32)


def dot_tn(a, b):
    return lax.dot_general(a, b, (((0,), (0,)), ((), ())), preferred_element_type=F32)


def split_pair(x):
    high = x.astype(BF16).astype(F32)
    return high, x - high


def normalise(raw):
    factor = lax.rsqrt(jnp.mean(raw * raw, axis=-1, keepdims=True) + EPSILON)
    return factor, (raw * factor).astype(BF16)


def head_columns(j):
    return slice(j * HEAD_DIM, (j + 1) * HEAD_DIM)


def pack_kernel(me_ref, route_ref, qk_hbm, v_hbm, g_hbm, o_ref, qk_buf, v_buf, g_buf, sems):
    inputs = ((qk_hbm, qk_buf), (v_hbm, v_buf), (g_hbm, g_buf))

    def copies(step):
        span = pl.ds(step * STEP_COLS, STEP_COLS)
        return [
            pltpu.make_async_copy(hbm.at[:, span], buf.at[:, span], sems.at[step, k])
            for k, (hbm, buf) in enumerate(inputs)
        ]

    for step in range(STEPS):
        for copy in copies(step):
            copy.start()

    me = me_ref[0]
    route = route_ref[...]
    own = route_ref[pl.ds(me, 1), :]
    tiles = lax.broadcasted_iota(jnp.int32, route.shape, 0)
    earlier = jnp.where((route == own) & (tiles < me), 1.0, 0.0)
    uppers = jnp.max(earlier, axis=0, keepdims=True)

    rows = lax.broadcasted_iota(jnp.int32, (TILE, TILE), 0)
    cols = lax.broadcasted_iota(jnp.int32, (TILE, TILE), 1)
    at_most = rows <= cols
    for j in range(HEADS):
        if j % STEP_HEADS == 0:
            for copy in copies(j // STEP_HEADS):
                copy.wait()
        upper = uppers[:, j : j + 1] > 0.0
        value = v_buf[:, head_columns(j)]
        grad = g_buf[:, head_columns(j)]
        _, normed = normalise(qk_buf[:, head_columns(j)].astype(F32))
        weights = jnp.where(at_most, jnp.exp(dot_nt(normed, normed) * SCALE), 0.0)
        grad_probs = dot_nt(value, grad)
        total = jnp.sum(weights, axis=0, keepdims=True)
        moment = jnp.sum(weights * grad_probs, axis=0, keepdims=True)
        stats = jnp.concatenate(
            [*split_pair(total), *split_pair(moment), jnp.zeros((4, TILE), F32)], axis=0
        ).astype(BF16)
        second = jnp.where(upper, grad.astype(F32), value.astype(F32)).astype(BF16)
        o_ref[j, :, 0:ROWS, :] = normed.reshape(SLICES, ROWS, HEAD_DIM)
        o_ref[j, :, ROWS : 2 * ROWS, :] = second.reshape(SLICES, ROWS, HEAD_DIM)
        o_ref[j, :, 2 * ROWS : MSG, :] = jnp.broadcast_to(
            stats[None], (SLICES, MSG - 2 * ROWS, TILE)
        )


def pack(me, route, qk, value, grad):
    buffer = pltpu.VMEM((TILE, HEADS * HEAD_DIM), BF16)
    hbm = pl.BlockSpec(memory_space=pltpu.HBM)
    whole = pl.BlockSpec(memory_space=pltpu.VMEM)
    return pl.pallas_call(
        pack_kernel,
        out_shape=jax.ShapeDtypeStruct((HEADS, SLICES, MSG, HEAD_DIM), BF16),
        in_specs=[pl.BlockSpec(memory_space=pltpu.SMEM), whole, hbm, hbm, hbm],
        out_specs=whole,
        scratch_shapes=[buffer, buffer, buffer, pltpu.SemaphoreType.DMA((STEPS, 3))],
        compiler_params=pltpu.CompilerParams(vmem_limit_bytes=16 * 1024 * 1024),
        name="pack",
    )(me, route, qk, value, grad)


def swap_kernel(partner_ref, x_ref, o_ref):
    def move(t, carry):
        o_ref[t] = x_ref[partner_ref[t]]
        return carry

    lax.fori_loop(0, TILES, move, 0, unroll=8)


def swap(partner, x):
    whole = pl.BlockSpec(memory_space=pltpu.VMEM)
    return pl.pallas_call(
        swap_kernel,
        out_shape=jax.ShapeDtypeStruct(x.shape, x.dtype),
        in_specs=[pl.BlockSpec(memory_space=pltpu.SMEM), whole],
        out_specs=whole,
        compiler_params=pltpu.CompilerParams(vmem_limit_bytes=16 * 1024 * 1024),
        name="swap",
    )(partner, x)


def finish_kernel(upper_ref, qk_ref, v_ref, g_ref, z_ref, out_ref, dqk_ref, dv_ref):
    rows = lax.broadcasted_iota(jnp.int32, (TILE, TILE), 0)
    cols = lax.broadcasted_iota(jnp.int32, (TILE, TILE), 1)
    causal = cols <= rows
    for j in range(HEADS):
        upper = upper_ref[j] != 0
        value = v_ref[:, head_columns(j)]
        grad = g_ref[:, head_columns(j)]
        raw = qk_ref[:, head_columns(j)].astype(F32)
        factor, normed = normalise(raw)
        second = jnp.where(upper, grad, value)
        their_normed = z_ref[j, :, 0:ROWS, :].reshape(TILE, HEAD_DIM)
        their_second = z_ref[j, :, ROWS : 2 * ROWS, :].reshape(TILE, HEAD_DIM)
        stats = z_ref[j, 0, 2 * ROWS : MSG, :].astype(F32)
        their_total = stats[0:1] + stats[1:2]
        their_moment = stats[2:3] + stats[3:4]

        weights = jnp.where(causal, jnp.exp(dot_nt(normed, normed) * SCALE), 0.0)
        cross = jnp.exp(dot_nt(normed, their_normed) * SCALE)
        grad_probs = dot_nt(grad, value)
        cross_grad_probs = dot_nt(second, their_second)

        row_total = jnp.sum(weights, axis=1, keepdims=True)
        cross_row = jnp.sum(cross, axis=1, keepdims=True)
        inv_row = 1.0 / (row_total + jnp.where(upper, cross_row, 0.0))
        inv_col = 1.0 / (their_total + jnp.sum(cross, axis=0, keepdims=True))
        probs = (weights * inv_row).astype(BF16)
        cross_probs = (cross * jnp.where(upper, inv_row, inv_col)).astype(BF16)
        probs_f = probs.astype(F32)
        cross_f = cross_probs.astype(F32)
        cross_terms = cross_f * cross_grad_probs
        row_sum = jnp.sum(probs_f * grad_probs, axis=1, keepdims=True)
        row_sum += jnp.where(upper, jnp.sum(cross_terms, axis=1, keepdims=True), 0.0)
        col_sum = their_moment * inv_col + jnp.sum(cross_terms, axis=0, keepdims=True)
        scores = (probs_f * (grad_probs - row_sum) * SCALE).astype(BF16)
        cross_scores = (
            cross_f * (cross_grad_probs - jnp.where(upper, row_sum, col_sum)) * SCALE
        ).astype(BF16)

        mixed = dot_nn(cross_probs, their_second)
        out = dot_nn(probs, value) + jnp.where(upper, mixed, 0.0)
        grad_value = dot_tn(probs, grad) + jnp.where(upper, 0.0, mixed)
        grad_normed = (
            dot_nn(scores, normed) + dot_tn(scores, normed) + dot_nn(cross_scores, their_normed)
        )
        grad_normed = grad_normed.astype(BF16).astype(F32)
        grad_input = factor * grad_normed - raw * factor**3 * jnp.mean(
            raw * grad_normed, axis=-1, keepdims=True
        )
        out_ref[:, head_columns(j)] = out.astype(BF16)
        dqk_ref[:, head_columns(j)] = grad_input.astype(BF16)
        dv_ref[:, head_columns(j)] = grad_value.astype(BF16)


def finish(upper, qk, value, grad, z):
    shape = jax.ShapeDtypeStruct((TILE, HEADS * HEAD_DIM), BF16)
    whole = pl.BlockSpec(memory_space=pltpu.VMEM)
    return pl.pallas_call(
        finish_kernel,
        out_shape=(shape, shape, shape),
        in_specs=[pl.BlockSpec(memory_space=pltpu.SMEM), whole, whole, whole, whole],
        out_specs=(whole, whole, whole),
        compiler_params=pltpu.CompilerParams(vmem_limit_bytes=16 * 1024 * 1024),
        name="finish",
    )(upper, qk, value, grad, z)


def exchange(x):
    return lax.all_to_all(x, "seq", split_axis=0, concat_axis=0, tiled=True)


def local(query_key, payload_matrix, out_grad, route_assignment):
    me = lax.axis_index("seq")
    route = route_assignment[0]
    tiles = jnp.arange(TILES, dtype=jnp.int32)

    own = lax.dynamic_index_in_dim(route, me, 0, keepdims=True)
    upper = jnp.any((route == own) & (tiles[:, None] < me), axis=0).astype(jnp.int32)

    labels = lax.dynamic_index_in_dim(route, me // SLICES, 1, keepdims=False)
    same = (labels[:, None] == labels[None, :]) & (tiles[:, None] != tiles[None, :])
    partner = jnp.sum(jnp.where(same, tiles[:, None], 0), axis=0)

    packed = pack(me.reshape(1), route, query_key[0], payload_matrix[0], out_grad[0])
    slices = exchange(packed.reshape(TILES, MSG, HEAD_DIM))
    swapped = swap(partner, slices)
    theirs = exchange(swapped).reshape(HEADS, SLICES, MSG, HEAD_DIM)
    out, grad_qk, grad_v = finish(upper, query_key[0], payload_matrix[0], out_grad[0], theirs)
    pairs = [(0, 1), (1, 0)]
    grad_qk, grad_v = lax.ppermute((grad_qk, grad_v), "pipe", pairs)
    return (out[None], grad_qk[None], grad_v[None])


def solution(mesh):
    rows = P("pipe", "seq", None)
    return jax.shard_map(
        local,
        mesh=mesh,
        in_specs=(rows, rows, rows, P("pipe", None, None)),
        out_specs=(rows, rows, rows),
        check_vma=False,
    )
```

time: 748 us -> 117 us (0.16)
  waiting for transfers between devices: 498 us -> 67.1 us
  local copies, waits for them, and re-layouts: 83.3 us -> 5.71 us
  starting transfers between devices: 75.4 us -> 30.1 us
  matrix products: 43.4 us -> 0 us
  other arithmetic: 40.7 us -> 0.22 us
  Pallas kernels: 0 us -> 12.3 us
    all_to_all x6 -> x2, waiting for transfers between devices: 498 us -> 64.9 us  [exchange(): return lax.all_to_all(x, 'seq', split_axis=0, concat_axis=0, tiled=True)]
    all_to_all x6 -> x2, starting transfers between devices: 73.4 us -> 25.8 us  [exchange(): return lax.all_to_all(x, 'seq', split_axis=0, concat_axis=0, tiled=True)]
    dot_general x48 -> x0, matrix products: 43.4 us -> none  [the longest x8 14.4 us: cluster_backward(): jnp.dot(attn_probs.T, grad_rows, preferred_element_type=jnp.float32)]
    gather x13 -> x0, local copies, waits for them, and re-layouts: 34.4 us -> none  [the longest x3 13.7 us: local(): dest_all = keeper_register[reader_roster[None, :], cluster_labels]]
    another operation x1 -> x0, other arithmetic: 23.6 us -> none  [cluster_members(): rank_pos = jnp.cumsum(hit_mask.astype(jnp.int32)) - 1]
    another operation x9 -> x0, local copies, waits for them, and re-layouts: 19.8 us -> none
    scatter x6 -> x0, local copies, waits for them, and re-layouts: 15.5 us -> none  [the longest x3 7.74 us: pack_send(): return empty.at[send_rows].set(item_block)]
    pallas_call x0 -> x3, Pallas kernels: none -> 12.3 us  [the longest x1 7.38 us: finish(): pl.pallas_call(finish_kernel, out_shape=(shape, shape, shape), in_specs=[...]
  transfers between devices with their start and end apart: 8 -> 4, of which waited for: 6 -> 4; matrix products, arithmetic and copies ran while one was open for 8% -> 0% of each run, Pallas kernels for 0% -> 0%
where the time goes in v1:
time: 117 us; the launch traced here: 116 us
  waiting for transfers between devices  67.1 us (57%)
  starting transfers between devices  30.1 us (26%)
  Pallas kernels  12.3 us (11%)
  local copies, waits for them, and re-layouts  5.71 us (5%)
    all_to_all x2, waiting for transfers between devices, exchange(): return lax.all_to_all(x, 'seq', split_axis=0, concat_axis=0, tiled=True)  64.9 us
    all_to_all x2, starting transfers between devices, exchange(): return lax.all_to_all(x, 'seq', split_axis=0, concat_axis=0, tiled=True)  25.8 us
    pallas_call x1, Pallas kernels, finish(): pl.pallas_call(finish_kernel, out_shape=(shape, shape, shape), in_specs=[...  7.38 us
    unnamed x17, local copies, waits for them, and re-layouts  5.52 us
    ppermute x2, starting transfers between devices, local(): grad_qk, grad_v = lax.ppermute((grad_qk, grad_v), 'pipe', pairs)  4.26 us
    pallas_call x1, Pallas kernels, pack(): pl.pallas_call(pack_kernel, out_shape=jax.ShapeDtypeStruct((HEADS, SLICES...  3.11 us
  transfers between devices with their start and end apart: 4, of which 4 were waited for; matrix products, arithmetic and copies ran while one was open for 0% of the time, Pallas kernels for 0%

profile of v1, /device:TPU:1, one launch (start us, length us, event | category | flops | bytes accessed | tf_op | source)
XLA Modules:
  0.0 116.2 jit_solution(17661532463034854571)
XLA Ops:
  0.6 0.8 copy.9
  1.4 0.0 copy-start
  1.4 1.0 copy-done
  2.5 0.0 copy-start.2
  2.5 1.0 copy-done.2
  3.5 0.0 copy-start.4
  3.5 1.0 copy-done.4
  4.6 3.1 %pack.1 = bf16[16,8,40,128]{3,2,1,0:T(8,128)(2,1)} custom-call(s32[1]{0:T(128)} %bitcast.5.me_ref, s32[128,16]{1,0:T(8,128)S(1)} %bitcast.20, bf16[128,2048]{1,0:T(8,128)(2,1)S(1)} %bitcast.14, bf16[128,2048]{1,0:T(8,128)(2,1)S(1)} %bitcast.16, bf16[128,2048]{1,0:T(8,128)(2,1)S(1)} %bitcast.18), custom_call_target="tpu_custom_call" | custom-call | tf_op jit(solution)/shard_map/pack/pallas_call | solution.py:101
  7.7 0.0 copy-start.6
  7.7 16.3 %all-to-all-start = ((bf16[128,40,128]{2,1,0:T(8,128)(2,1)}), bf16[128,40,128]{2,1,0:T(8,128)(2,1)S(1)}, u32[]{:S(2)}, u32[]{:S(2)}) async-start(bf16[128,40,128]{2,1,0:T(8,128)(2,1)} %bitcast.6), calls=%async_computation | async-start | bytes 2621440 | tf_op jit(solution)/shard_map/all_to_all | solution.py:200
  24.1 0.0 copy-done.6
  24.1 0.1 select_reduce_fusion.partner_ref
  24.2 32.8 %all-to-all-done.x_ref = bf16[128,40,128]{2,1,0:T(8,128)(2,1)S(1)} async-done(((bf16[128,40,128]{2,1,0:T(8,128)(2,1)}), bf16[128,40,128]{2,1,0:T(8,128)(2,1)S(1)}, u32[]{:S(2)}, u32[]{:S(2)}) %all-to-all-start) | async-done | bytes 1310752 | tf_op jit(solution)/shard_map/all_to_all | solution.py:200
  57.0 1.8 %swap.1 = bf16[128,40,128]{2,1,0:T(8,128)(2,1)} custom-call(s32[128]{0:T(128)S(1)} %select_reduce_fusion.partner_ref, bf16[128,40,128]{2,1,0:T(8,128)(2,1)S(1)} %all-to-all-done.x_ref), custom_call_target="tpu_custom_call" | custom-call | tf_op jit(solution)/shard_map/swap/pallas_call | solution.py:122
  58.8 0.0 copy-start.1
  58.8 0.0 copy-start.3
  58.8 0.0 copy-start.5
  58.8 9.5 %all-to-all-start.1 = ((bf16[128,40,128]{2,1,0:T(8,128)(2,1)}), bf16[128,40,128]{2,1,0:T(8,128)(2,1)S(1)}, u32[]{:S(2)}, u32[]{:S(2)}) async-start(bf16[128,40,128]{2,1,0:T(8,128)(2,1)} %swap.1), calls=%async_computation.1 | async-start | bytes 2621440 | tf_op jit(solution)/shard_map/all_to_all | solution.py:200
  68.4 0.2 dynamic-slice_reduce_fusion
  68.5 0.1 and_reduce_fusion
  68.7 32.0 %all-to-all-done.1 = bf16[128,40,128]{2,1,0:T(8,128)(2,1)S(1)} async-done(((bf16[128,40,128]{2,1,0:T(8,128)(2,1)}), bf16[128,40,128]{2,1,0:T(8,128)(2,1)S(1)}, u32[]{:S(2)}, u32[]{:S(2)}) %all-to-all-start.1) | async-done | bytes 1310752 | tf_op jit(solution)/shard_map/all_to_all | solution.py:200
  100.7 0.0 copy-done.1
  100.7 0.0 copy-done.3
  100.7 0.0 copy-done.5
  100.7 7.4 %finish.1 = (bf16[128,2048]{1,0:T(8,128)(2,1)}, bf16[128,2048]{1,0:T(8,128)(2,1)S(1)}, bf16[128,2048]{1,0:T(8,128)(2,1)S(1)}) custom-call(s32[16]{0:T(128)S(1)} %convert_element_type.3.upper_ref, bf16[128,2048]{1,0:T(8,128)(2,1)S(1)} %bitcast.15, bf16[128,2048]{1,0:T(8,128)(2,1)S(1)} %bitcast.17, bf16[128,2048]{1,0:T(8,128)(2,1)S(1)} %bitcast.19, ...), custom_call_target="tpu_custom_call" | custom-call | tf_op jit(solution)/shard_map/finish/pallas_call | solution.py:189
  108.1 4.3 %collective-permute-start = (bf16[128,2048]{1,0:T(8,128)(2,1)S(1)}, bf16[128,2048]{1,0:T(8,128)(2,1)S(1)}, u32[]{:S(2)}, u32[]{:S(2)}) collective-permute-start(bf16[128,2048]{1,0:T(8,128)(2,1)S(1)} %get-tuple-element.7), channel_id=1, source_target_pairs={{0,1},{1,0},{2,3},{3,2},{4,5},{5,4},{6,7},{7,6},{8,9},{9,8},{10,11... | collective-permute-start | bytes 1572872 | tf_op jit(solution)/shard_map/ppermute | solution.py:221
  112.4 0.0 collective-permute-start.1
  112.4 1.5 %collective-permute-done = bf16[128,2048]{1,0:T(8,128)(2,1)S(1)} collective-permute-done((bf16[128,2048]{1,0:T(8,128)(2,1)S(1)}, bf16[128,2048]{1,0:T(8,128)(2,1)S(1)}, u32[]{:S(2)}, u32[]{:S(2)}) %collective-permute-start) | collective-permute-done | bytes 524320 | tf_op jit(solution)/shard_map/ppermute | solution.py:221
  113.9 0.7 collective-permute-done.1
  114.6 0.8 copy.12
  115.4 0.8 copy.13
  (3 shorter events, 0.0 us)
Async XLA Ops:
  1.4 1.0 copy-start
  2.5 1.0 copy-start.2
  3.5 1.0 copy-start.4
  7.7 16.4 %copy-start.6 = (s32[1,128,16]{1,2,0:T(8,128)S(1)}, s32[1,128,16]{1,2,0:T(8,128)}, u32[]{:S(2)}) copy-start(s32[1,128,16]{1,2,0:T(8,128)} %param.7) | copy-start | bytes 24580
  7.7 49.3 %all-to-all-start = ((bf16[128,40,128]{2,1,0:T(8,128)(2,1)}), bf16[128,40,128]{2,1,0:T(8,128)(2,1)S(1)}, u32[]{:S(2)}, u32[]{:S(2)}) async-start(bf16[128,40,128]{2,1,0:T(8,128)(2,1)} %bitcast.6), calls=%async_computation | async-start | bytes 2621440 | tf_op jit(solution)/shard_map/all_to_all | solution.py:200
  58.8 41.9 %copy-start.1 = (bf16[1,128,2048]{2,1,0:T(8,128)(2,1)S(1)}, bf16[1,128,2048]{2,1,0:T(8,128)(2,1)}, u32[]{:S(2)}) copy-start(bf16[1,128,2048]{2,1,0:T(8,128)(2,1)} %param.4) | copy-start | bytes 1572868
  58.8 41.9 %copy-start.3 = (bf16[1,128,2048]{2,1,0:T(8,128)(2,1)S(1)}, bf16[1,128,2048]{2,1,0:T(8,128)(2,1)}, u32[]{:S(2)}) copy-start(bf16[1,128,2048]{2,1,0:T(8,128)(2,1)} %param.5) | copy-start | bytes 1572868
  58.8 41.9 %copy-start.5 = (bf16[1,128,2048]{2,1,0:T(8,128)(2,1)S(1)}, bf16[1,128,2048]{2,1,0:T(8,128)(2,1)}, u32[]{:S(2)}) copy-start(bf16[1,128,2048]{2,1,0:T(8,128)(2,1)} %param.6) | copy-start | bytes 1572868
  58.8 41.9 %all-to-all-start.1 = ((bf16[128,40,128]{2,1,0:T(8,128)(2,1)}), bf16[128,40,128]{2,1,0:T(8,128)(2,1)S(1)}, u32[]{:S(2)}, u32[]{:S(2)}) async-start(bf16[128,40,128]{2,1,0:T(8,128)(2,1)} %swap.1), calls=%async_computation.1 | async-start | bytes 2621440 | tf_op jit(solution)/shard_map/all_to_all | solution.py:200
  108.1 5.8 %collective-permute-start = (bf16[128,2048]{1,0:T(8,128)(2,1)S(1)}, bf16[128,2048]{1,0:T(8,128)(2,1)S(1)}, u32[]{:S(2)}, u32[]{:S(2)}) collective-permute-start(bf16[128,2048]{1,0:T(8,128)(2,1)S(1)} %get-tuple-element.7), channel_id=1, source_target_pairs={{0,1},{1,0},{2,3},{3,2},{4,5},{5,4},{6,7},{7,6},{8,9},{9,8},{10,11... | collective-permute-start | bytes 1572872 | tf_op jit(solution)/shard_map/ppermute | solution.py:221
  112.4 2.3 %collective-permute-start.1 = (bf16[128,2048]{1,0:T(8,128)(2,1)S(1)}, bf16[128,2048]{1,0:T(8,128)(2,1)S(1)}, u32[]{:S(2)}, u32[]{:S(2)}) collective-permute-start(bf16[128,2048]{1,0:T(8,128)(2,1)S(1)} %get-tuple-element.8), channel_id=1, source_target_pairs={{0,1},{1,0},{2,3},{3,2},{4,5},{5,4},{6,7},{7,6},{8,9},{9,8},{10,11... | collective-permute-start | bytes 1572872 | tf_op jit(solution)/shard_map/ppermute | solution.py:221

commit v2 on v1

v2 whole, which is shorter than its diff:
```python
import jax
import jax.numpy as jnp
from jax import lax
from jax.experimental import pallas as pl
from jax.experimental.pallas import tpu as pltpu
from jax.sharding import PartitionSpec as P

HEADS = 16
HEAD_DIM = 128
TILE = 128
TILES = 128
SLICES = 8
PAIRS = TILE // SLICES // 2
MSG = 2 * PAIRS + 1
STEP_HEADS = 4
SWAP_STEPS = 4
STEPS = HEADS // STEP_HEADS
STEP_COLS = STEP_HEADS * HEAD_DIM
EPSILON = 1e-06
SCALE = 4.0 / HEAD_DIM
F32 = jnp.float32
BF16 = jnp.bfloat16
GROUP = 8
VMEM_LIMIT = 16 * 1024 * 1024


def dot_nt(a, b):
    return lax.dot_general(a, b, (((1,), (1,)), ((), ())), preferred_element_type=F32)


def dot_nn(a, b):
    return lax.dot_general(a, b, (((1,), (0,)), ((), ())), preferred_element_type=F32)


def dot_tn(a, b):
    return lax.dot_general(a, b, (((0,), (0,)), ((), ())), preferred_element_type=F32)


def split_pair(x):
    high = x.astype(BF16).astype(F32)
    return high, x - high


def normalise(raw):
    factor = lax.rsqrt(jnp.mean(raw * raw, axis=-1, keepdims=True) + EPSILON)
    return factor, (raw * factor).astype(BF16)


def head_columns(j):
    return slice(j * HEAD_DIM, (j + 1) * HEAD_DIM)


def grid_of(axis):
    return lax.broadcasted_iota(jnp.int32, (TILE, TILE), axis)


def pick(upper, if_upper, if_lower):
    return jnp.where(upper, if_upper.astype(F32), if_lower.astype(F32)).astype(BF16)


def in_step(heads):
    while heads:
        heads = [head for head in heads if next(head, head) is not head]


def pack_kernel(me_ref, route_hbm, qk_hbm, v_hbm, g_hbm, o_hbm, route_buf, o_buf, *scratch):
    buffers, sems = scratch[:3], scratch[3]
    inputs = (qk_hbm, v_hbm, g_hbm)

    def loads(step):
        span = pl.ds(step * STEP_COLS, STEP_COLS)
        return [
            pltpu.make_async_copy(hbm.at[:, span], buf.at[:, span], sems.at[step, k])
            for k, (hbm, buf) in enumerate(zip(inputs, buffers))
        ]

    def store(step):
        span = pl.ds(step * STEP_HEADS, STEP_HEADS)
        return pltpu.make_async_copy(o_buf.at[span], o_hbm.at[span], sems.at[step, 3])

    route_load = pltpu.make_async_copy(route_hbm, route_buf, sems.at[STEPS, 0])
    route_load.start()
    for step in range(STEPS):
        for load in loads(step):
            load.start()
    qk_buf, v_buf, g_buf = buffers

    route_load.wait()
    me = me_ref[0]
    route = route_buf[...]
    tiles = lax.broadcasted_iota(jnp.int32, route.shape, 1)
    own = jnp.sum(jnp.where(tiles == me, route, 0), axis=1, keepdims=True)
    earlier = jnp.where((route == own) & (tiles < me), 1.0, 0.0)
    uppers = jnp.max(earlier, axis=1, keepdims=True)
    at_most = grid_of(0) <= grid_of(1)

    def head(j):
        upper = uppers[j : j + 1, :] > 0.0
        value = v_buf[:, head_columns(j)]
        grad = g_buf[:, head_columns(j)]
        _, normed = normalise(qk_buf[:, head_columns(j)].astype(F32))
        second = pick(upper, grad, value)
        o_buf[j, :, 0:PAIRS] = normed.reshape(SLICES, PAIRS, 2, HEAD_DIM)
        o_buf[j, :, PAIRS : 2 * PAIRS] = second.reshape(SLICES, PAIRS, 2, HEAD_DIM)
        yield
        weights = jnp.where(at_most, jnp.exp(dot_nt(normed, normed) * SCALE), 0.0)
        grad_probs = dot_nt(value, grad)
        yield
        total = jnp.sum(weights, axis=0, keepdims=True)
        moment = jnp.sum(weights * grad_probs, axis=0, keepdims=True)
        yield
        stats = jnp.concatenate(
            [*split_pair(total), *split_pair(moment), jnp.zeros((12, TILE), F32)], axis=0
        ).astype(BF16)
        o_buf[j, :, 2 * PAIRS] = stats.reshape(SLICES, 2, TILE)

    for step in range(STEPS):
        for load in loads(step):
            load.wait()
        in_step([head(step * STEP_HEADS + j) for j in range(STEP_HEADS)])
        store(step).start()
    for step in range(STEPS):
        store(step).wait()


def pack(me, route, qk, value, grad):
    shape = (HEADS, SLICES, MSG, 2, HEAD_DIM)
    buffer = pltpu.VMEM((TILE, HEADS * HEAD_DIM), BF16)
    hbm = pl.BlockSpec(memory_space=pltpu.HBM)
    return pl.pallas_call(
        pack_kernel,
        out_shape=pltpu.HBM(shape, BF16),
        in_specs=[pl.BlockSpec(memory_space=pltpu.SMEM), hbm, hbm, hbm, hbm],
        out_specs=hbm,
        scratch_shapes=[
            pltpu.VMEM((HEADS, TILES), jnp.int32),
            pltpu.VMEM(shape, BF16),
            buffer,
            buffer,
            buffer,
            pltpu.SemaphoreType.DMA((STEPS + 1, 4)),
        ],
        compiler_params=pltpu.CompilerParams(vmem_limit_bytes=VMEM_LIMIT),
        name="pack",
    )(me, *[pltpu.with_memory_space_constraint(x, pltpu.HBM) for x in (route, qk, value, grad)])


def swap_kernel(partner_ref, x_ref, o_hbm, o_buf, sems):
    count = TILES // SWAP_STEPS

    def store(step):
        span = pl.ds(step * count, count)
        return pltpu.make_async_copy(o_buf.at[span], o_hbm.at[span], sems.at[step])

    def move(t, carry):
        o_buf[t] = x_ref[partner_ref[t]]
        return carry

    for step in range(SWAP_STEPS):
        lax.fori_loop(step * count, (step + 1) * count, move, 0, unroll=16)
        store(step).start()
    for step in range(SWAP_STEPS):
        store(step).wait()


def swap(partner, x):
    return pl.pallas_call(
        swap_kernel,
        out_shape=pltpu.HBM(x.shape, x.dtype),
        in_specs=[
            pl.BlockSpec(memory_space=pltpu.SMEM),
            pl.BlockSpec(memory_space=pltpu.VMEM),
        ],
        out_specs=pl.BlockSpec(memory_space=pltpu.HBM),
        scratch_shapes=[pltpu.VMEM(x.shape, x.dtype), pltpu.SemaphoreType.DMA((SWAP_STEPS,))],
        compiler_params=pltpu.CompilerParams(vmem_limit_bytes=VMEM_LIMIT),
        name="swap",
    )(partner, x)


def attend_kernel(
    upper_ref, qk_ref, v_ref, g_ref, z_ref, out_hbm, dv_ref, scores_ref, out_buf, sems
):
    def store(step):
        span = pl.ds(step * STEP_COLS, STEP_COLS)
        return pltpu.make_async_copy(out_buf.at[:, span], out_hbm.at[:, span], sems.at[step])

    ahead = grid_of(0) - grid_of(1)

    def head(j):
        upper = upper_ref[j] != 0
        value = v_ref[:, head_columns(j)]
        grad = g_ref[:, head_columns(j)]
        _, normed = normalise(qk_ref[:, head_columns(j)].astype(F32))
        second = pick(upper, grad, value)
        first = pick(upper, value, grad)
        their_normed = z_ref[j, :, 0:PAIRS].reshape(TILE, HEAD_DIM)
        their_second = z_ref[j, :, PAIRS : 2 * PAIRS].reshape(TILE, HEAD_DIM)
        stats = z_ref[j, :, 2 * PAIRS].reshape(2 * SLICES, TILE).astype(F32)
        their_total = stats[0:1] + stats[1:2]
        their_moment = stats[2:3] + stats[3:4]
        keys = jnp.concatenate([normed, their_normed], axis=0)
        others = jnp.concatenate([first, their_second], axis=0)
        yield
        weights = jnp.exp(dot_nt(normed, keys) * SCALE)
        grad_probs = dot_nt(second, others)
        yield
        inside = jnp.where(upper, ahead, -ahead) >= 0
        own_w = jnp.where(inside, weights[:, :TILE], 0.0)
        cross_w = weights[:, TILE:]
        own_g = grad_probs[:, :TILE]
        cross_g = grad_probs[:, TILE:]
        inv_row = 1.0 / jnp.sum(own_w + cross_w, axis=1, keepdims=True)
        own_inv = 1.0 / jnp.sum(own_w, axis=0, keepdims=True)
        cross_inv = 1.0 / (their_total + jnp.sum(cross_w, axis=0, keepdims=True))
        yield
        own_p = (own_w * jnp.where(upper, inv_row, own_inv)).astype(BF16)
        cross_p = (cross_w * jnp.where(upper, inv_row, cross_inv)).astype(BF16)
        own_f = own_p.astype(F32)
        cross_f = cross_p.astype(F32)
        own_t = own_f * own_g
        cross_t = cross_f * cross_g
        yield
        row_sum = jnp.sum(own_t + cross_t, axis=1, keepdims=True)
        own_sum = jnp.sum(own_t, axis=0, keepdims=True)
        cross_sum = their_moment * cross_inv + jnp.sum(cross_t, axis=0, keepdims=True)
        yield
        own_s = own_f * (own_g - jnp.where(upper, row_sum, own_sum)) * SCALE
        cross_s = cross_f * (cross_g - jnp.where(upper, row_sum, cross_sum)) * SCALE
        scores_ref[j, :, :TILE] = own_s.astype(BF16)
        scores_ref[j, :, TILE:] = cross_s.astype(BF16)
        along = dot_nn(jnp.concatenate([own_p, cross_p], axis=1), others)
        across = dot_tn(own_p, second)
        yield
        out_buf[:, head_columns(j)] = jnp.where(upper, along, across).astype(BF16)
        dv_ref[:, head_columns(j)] = jnp.where(upper, across, along).astype(BF16)

    for start in range(0, HEADS, GROUP):
        in_step([head(start + j) for j in range(GROUP)])
        for step in range(start // STEP_HEADS, (start + GROUP) // STEP_HEADS):
            store(step).start()
    for step in range(STEPS):
        store(step).wait()


def attend(upper, qk, value, grad, z):
    shape = jax.ShapeDtypeStruct((TILE, HEADS * HEAD_DIM), BF16)
    scores = jax.ShapeDtypeStruct((HEADS, TILE, 2 * TILE), BF16)
    whole = pl.BlockSpec(memory_space=pltpu.VMEM)
    return pl.pallas_call(
        attend_kernel,
        out_shape=(pltpu.HBM(shape.shape, shape.dtype), shape, scores),
        in_specs=[pl.BlockSpec(memory_space=pltpu.SMEM)] + [whole] * 4,
        out_specs=(pl.BlockSpec(memory_space=pltpu.HBM), whole, whole),
        scratch_shapes=[pltpu.VMEM(shape.shape, BF16), pltpu.SemaphoreType.DMA((STEPS,))],
        compiler_params=pltpu.CompilerParams(vmem_limit_bytes=VMEM_LIMIT),
        name="attend",
    )(upper, qk, value, grad, z)


def input_grad_kernel(qk_ref, z_ref, scores_ref, dqk_ref):
    def head(j):
        raw = qk_ref[:, head_columns(j)].astype(F32)
        factor, normed = normalise(raw)
        their_normed = z_ref[j, :, 0:PAIRS].reshape(TILE, HEAD_DIM)
        keys = jnp.concatenate([normed, their_normed], axis=0)
        yield
        grad_normed = dot_nn(scores_ref[j], keys) + dot_tn(scores_ref[j, :, :TILE], normed)
        grad_normed = grad_normed.astype(BF16).astype(F32)
        yield
        inner = jnp.mean(raw * grad_normed, axis=-1, keepdims=True)
        grad_input = factor * grad_normed - raw * (factor**3 * inner)
        dqk_ref[:, head_columns(j)] = grad_input.astype(BF16)

    for start in range(0, HEADS, GROUP):
        in_step([head(start + j) for j in range(GROUP)])


def input_grad(qk, z, scores):
    whole = pl.BlockSpec(memory_space=pltpu.VMEM)
    return pl.pallas_call(
        input_grad_kernel,
        out_shape=jax.ShapeDtypeStruct((TILE, HEADS * HEAD_DIM), BF16),
        in_specs=[whole] * 3,
        out_specs=whole,
        compiler_params=pltpu.CompilerParams(vmem_limit_bytes=VMEM_LIMIT),
        cost_estimate=pl.CostEstimate(
            flops=HEADS * 6 * TILE * TILE * HEAD_DIM, bytes_accessed=3 * 1024 * 1024, transcendentals=0
        ),
        name="input_grad",
    )(qk, z, scores)


def exchange(x):
    return lax.all_to_all(x, "seq", split_axis=0, concat_axis=0, tiled=True)


def local(query_key, payload_matrix, out_grad, route_assignment):
    me = lax.axis_index("seq")
    route = route_assignment[0]
    rows = (query_key[0], payload_matrix[0], out_grad[0])
    tiles = jnp.arange(TILES, dtype=jnp.int32)

    own = lax.dynamic_index_in_dim(route, me, 0, keepdims=True)
    upper = jnp.any((route == own) & (tiles[:, None] < me), axis=0).astype(jnp.int32)

    labels = lax.dynamic_index_in_dim(route, me // SLICES, 1, keepdims=False)
    same = (labels[:, None] == labels[None, :]) & (tiles[:, None] != tiles[None, :])
    partner = jnp.sum(jnp.where(same, tiles[:, None], 0), axis=0)

    packed = pack(me.reshape(1), route.T, *rows)
    slices = exchange(packed.reshape(TILES, MSG, 2, HEAD_DIM))
    theirs = exchange(swap(partner, slices)).reshape(HEADS, SLICES, MSG, 2, HEAD_DIM)
    out, grad_v, scores = attend(upper, *rows, theirs)
    pairs = [(0, 1), (1, 0)]
    grad_v = lax.ppermute(grad_v, "pipe", pairs)
    grad_qk = lax.ppermute(input_grad(rows[0], theirs, scores), "pipe", pairs)
    return (out[None], grad_qk[None], grad_v[None])


def solution(mesh):
    rows = P("pipe", "seq", None)
    return jax.shard_map(
        local,
        mesh=mesh,
        in_specs=(rows, rows, rows, P("pipe", None, None)),
        out_specs=(rows, rows, rows),
        check_vma=False,
    )
```

time: 117 us -> 102 us (0.87)
  waiting for transfers between devices: 67.1 us -> 57.8 us
  local copies, waits for them, and re-layouts: 5.71 us -> 1.81 us
  Pallas kernels: 12.3 us -> 10.5 us
    all_to_all x2, waiting for transfers between devices: 64.9 us -> 55.6 us  [exchange(): return lax.all_to_all(x, 'seq', split_axis=0, concat_axis=0, tiled=True)]
    unnamed x17 -> x10, local copies, waits for them, and re-layouts: 5.52 us -> 1.61 us
    pallas_call x3 -> x4, Pallas kernels: 12.3 us -> 10.5 us  [the longest x1 3.98 us: attend(): pl.pallas_call(attend_kernel, out_shape=(pltpu.HBM(shape.shape, shape.dty...]
where the time goes in v2:
time: 102 us
  waiting for transfers between devices  57.8 us (57%)
  starting transfers between devices  30.7 us (30%)
  Pallas kernels  10.5 us (10%)
  local copies, waits for them, and re-layouts  1.81 us (2%)
    all_to_all x2, waiting for transfers between devices, exchange(): return lax.all_to_all(x, 'seq', split_axis=0, concat_axis=0, tiled=True)  55.6 us
    all_to_all x2, starting transfers between devices, exchange(): return lax.all_to_all(x, 'seq', split_axis=0, concat_axis=0, tiled=True)  25.8 us
    ppermute x1, starting transfers between devices, local(): grad_qk = lax.ppermute(input_grad(rows[0], theirs, scores), 'pipe', pairs)  4.79 us
    pallas_call x1, Pallas kernels, attend(): pl.pallas_call(attend_kernel, out_shape=(pltpu.HBM(shape.shape, shape.dty...  3.98 us
    pallas_call x1, Pallas kernels, pack(): pl.pallas_call(pack_kernel, out_shape=pltpu.HBM(shape, BF16), in_specs=[p...  3.7 us
  transfers between devices with their start and end apart: 4, of which 4 were waited for; matrix products, arithmetic and copies ran while one was open for 0% of the time, Pallas kernels for 0%

profile of v2, /device:TPU:1, one launch (start us, length us, event | category | flops | bytes accessed | tf_op | source)
XLA Modules:
  0.0 101.8 jit_solution(403088265629876997)
XLA Ops:
  0.6 3.7 %pack.1 = bf16[16,8,17,2,128]{4,3,2,1,0:T(2,128)(2,1)} custom-call(s32[1]{0:T(128)} %bitcast.5.me_ref, s32[16,128]{1,0:T(8,128)} %bitcast.31, bf16[128,2048]{1,0:T(8,128)(2,1)} %bitcast.21, bf16[128,2048]{1,0:T(8,128)(2,1)} %bitcast.24, bf16[128,2048]{1,0:T(8,128)(2,1)} %bitcast.26), custom_call_target="tpu_custom_call" | custom-call | tf_op jit(solution)/shard_map/pack/pallas_call | solution.py:130
  4.3 0.0 copy-start.3
  4.4 16.3 %all-to-all-start = ((bf16[128,17,2,128]{3,2,1,0:T(2,128)(2,1)}), bf16[128,17,2,128]{3,2,1,0:T(2,128)(2,1)S(1)}, u32[]{:S(2)}, u32[]{:S(2)}) async-start(bf16[128,17,2,128]{3,2,1,0:T(2,128)(2,1)} %bitcast.28), calls=%async_computation | async-start | bytes 2228224 | tf_op jit(solution)/shard_map/all_to_all | solution.py:295
  20.7 0.0 copy-done.3
  20.8 0.1 select_reduce_fusion.partner_ref
  20.9 28.4 %all-to-all-done.x_ref = bf16[128,17,2,128]{3,2,1,0:T(2,128)(2,1)S(1)} async-done(((bf16[128,17,2,128]{3,2,1,0:T(2,128)(2,1)}), bf16[128,17,2,128]{3,2,1,0:T(2,128)(2,1)S(1)}, u32[]{:S(2)}, u32[]{:S(2)}) %all-to-all-start) | async-done | bytes 1114144 | tf_op jit(solution)/shard_map/all_to_all | solution.py:295
  49.2 1.6 %swap.1 = bf16[128,17,2,128]{3,2,1,0:T(2,128)(2,1)} custom-call(s32[128]{0:T(128)S(1)} %select_reduce_fusion.partner_ref, bf16[128,17,2,128]{3,2,1,0:T(2,128)(2,1)S(1)} %all-to-all-done.x_ref), custom_call_target="tpu_custom_call" | custom-call | tf_op jit(solution)/shard_map/swap/pallas_call | solution.py:167
  50.9 0.0 copy-start
  50.9 0.0 copy-start.1
  50.9 0.0 copy-start.2
  50.9 9.4 %all-to-all-start.1 = ((bf16[128,17,2,128]{3,2,1,0:T(2,128)(2,1)}), bf16[128,17,2,128]{3,2,1,0:T(2,128)(2,1)S(1)}, u32[]{:S(2)}, u32[]{:S(2)}) async-start(bf16[128,17,2,128]{3,2,1,0:T(2,128)(2,1)} %swap.1), calls=%async_computation.1 | async-start | bytes 2228224 | tf_op jit(solution)/shard_map/all_to_all | solution.py:295
  60.3 0.2 dynamic-slice_reduce_fusion
  60.5 0.2 fusion.2
  60.7 27.3 %all-to-all-done.1 = bf16[128,17,2,128]{3,2,1,0:T(2,128)(2,1)S(1)} async-done(((bf16[128,17,2,128]{3,2,1,0:T(2,128)(2,1)}), bf16[128,17,2,128]{3,2,1,0:T(2,128)(2,1)S(1)}, u32[]{:S(2)}, u32[]{:S(2)}) %all-to-all-start.1) | async-done | bytes 1114144 | tf_op jit(solution)/shard_map/all_to_all | solution.py:295
  88.0 0.0 copy-done
  88.0 0.0 copy-done.1
  88.0 0.0 copy-done.2
  88.0 4.0 %attend.1 = (bf16[128,2048]{1,0:T(8,128)(2,1)}, bf16[128,2048]{1,0:T(8,128)(2,1)S(1)}, bf16[16,128,256]{2,1,0:T(8,128)(2,1)S(1)}) custom-call(s32[16]{0:T(128)S(1)} %convert_element_type.3.upper_ref, bf16[128,2048]{1,0:T(8,128)(2,1)S(1)} %bitcast.22, bf16[128,2048]{1,0:T(8,128)(2,1)S(1)} %bitcast.25, bf16[128,2048]{1,0:T(8,128)(2,1)S(1)} %bitcast.27, ...), custom_call_target="tpu_custom_call" | custom-call | tf_op jit(solution)/shard_map/attend/pallas_call | solution.py:250
  92.0 1.2 %input_grad.1 = bf16[128,2048]{1,0:T(8,128)(2,1)S(1)} custom-call(bf16[128,2048]{1,0:T(8,128)(2,1)S(1)} %bitcast.23, bf16[16,8,17,2,128]{4,3,2,1,0:T(2,128)(2,1)S(1)} %bitcast.20, bf16[16,128,256]{2,1,0:T(8,128)(2,1)S(1)} %get-tuple-element.7.scores_ref), custom_call_target="tpu_custom_call" | custom-call | flops 201326592 | bytes 3145728 | tf_op jit(solution)/shard_map/input_grad/pallas_call | solution.py:281
  93.1 4.8 %collective-permute-start = (bf16[128,2048]{1,0:T(8,128)(2,1)S(1)}, bf16[128,2048]{1,0:T(8,128)(2,1)S(1)}, u32[]{:S(2)}, u32[]{:S(2)}) collective-permute-start(bf16[128,2048]{1,0:T(8,128)(2,1)S(1)} %input_grad.1), channel_id=1, source_target_pairs={{0,1},{1,0},{2,3},{3,2},{4,5},{5,4},{6,7},{7,6},{8,9},{9,8},{10,11... | collective-permute-start | bytes 1572872 | tf_op jit(solution)/shard_map/ppermute | solution.py:317
  97.9 0.1 collective-permute-start.1
  98.0 1.4 %collective-permute-done = bf16[128,2048]{1,0:T(8,128)(2,1)S(1)} collective-permute-done((bf16[128,2048]{1,0:T(8,128)(2,1)S(1)}, bf16[128,2048]{1,0:T(8,128)(2,1)S(1)}, u32[]{:S(2)}, u32[]{:S(2)}) %collective-permute-start) | collective-permute-done | bytes 524320 | tf_op jit(solution)/shard_map/ppermute | solution.py:317
  99.4 0.7 collective-permute-done.1
  100.2 0.8 copy.9
  101.0 0.8 copy.10
  (3 shorter events, 0.0 us)
Async XLA Ops:
  4.3 16.4 %copy-start.3 = (s32[1,128,16]{1,2,0:T(8,128)S(1)}, s32[1,128,16]{1,2,0:T(8,128)}, u32[]{:S(2)}) copy-start(s32[1,128,16]{1,2,0:T(8,128)} %param.7) | copy-start | bytes 24580
  4.4 44.9 %all-to-all-start = ((bf16[128,17,2,128]{3,2,1,0:T(2,128)(2,1)}), bf16[128,17,2,128]{3,2,1,0:T(2,128)(2,1)S(1)}, u32[]{:S(2)}, u32[]{:S(2)}) async-start(bf16[128,17,2,128]{3,2,1,0:T(2,128)(2,1)} %bitcast.28), calls=%async_computation | async-start | bytes 2228224 | tf_op jit(solution)/shard_map/all_to_all | solution.py:295
  50.9 37.1 %copy-start = (bf16[1,128,2048]{2,1,0:T(8,128)(2,1)S(1)}, bf16[1,128,2048]{2,1,0:T(8,128)(2,1)}, u32[]{:S(2)}) copy-start(bf16[1,128,2048]{2,1,0:T(8,128)(2,1)} %param.4) | copy-start | bytes 1572868
  50.9 37.1 %copy-start.1 = (bf16[1,128,2048]{2,1,0:T(8,128)(2,1)S(1)}, bf16[1,128,2048]{2,1,0:T(8,128)(2,1)}, u32[]{:S(2)}) copy-start(bf16[1,128,2048]{2,1,0:T(8,128)(2,1)} %param.5) | copy-start | bytes 1572868
  50.9 37.1 %copy-start.2 = (bf16[1,128,2048]{2,1,0:T(8,128)(2,1)S(1)}, bf16[1,128,2048]{2,1,0:T(8,128)(2,1)}, u32[]{:S(2)}) copy-start(bf16[1,128,2048]{2,1,0:T(8,128)(2,1)} %param.6) | copy-start | bytes 1572868
  50.9 37.1 %all-to-all-start.1 = ((bf16[128,17,2,128]{3,2,1,0:T(2,128)(2,1)}), bf16[128,17,2,128]{3,2,1,0:T(2,128)(2,1)S(1)}, u32[]{:S(2)}, u32[]{:S(2)}) async-start(bf16[128,17,2,128]{3,2,1,0:T(2,128)(2,1)} %swap.1), calls=%async_computation.1 | async-start | bytes 2228224 | tf_op jit(solution)/shard_map/all_to_all | solution.py:295
  93.1 6.3 %collective-permute-start = (bf16[128,2048]{1,0:T(8,128)(2,1)S(1)}, bf16[128,2048]{1,0:T(8,128)(2,1)S(1)}, u32[]{:S(2)}, u32[]{:S(2)}) collective-permute-start(bf16[128,2048]{1,0:T(8,128)(2,1)S(1)} %input_grad.1), channel_id=1, source_target_pairs={{0,1},{1,0},{2,3},{3,2},{4,5},{5,4},{6,7},{7,6},{8,9},{9,8},{10,11... | collective-permute-start | bytes 1572872 | tf_op jit(solution)/shard_map/ppermute | solution.py:317
  97.9 2.3 %collective-permute-start.1 = (bf16[128,2048]{1,0:T(8,128)(2,1)S(1)}, bf16[128,2048]{1,0:T(8,128)(2,1)S(1)}, u32[]{:S(2)}, u32[]{:S(2)}) collective-permute-start(bf16[128,2048]{1,0:T(8,128)(2,1)S(1)} %get-tuple-element.8), channel_id=1, source_target_pairs={{0,1},{1,0},{2,3},{3,2},{4,5},{5,4},{6,7},{7,6},{8,9},{9,8},{10,11... | collective-permute-start | bytes 1572872 | tf_op jit(solution)/shard_map/ppermute | solution.py:316

commit v3 on v2

v3 whole, which is shorter than its diff:
```python
import math

import jax
import jax.numpy as jnp
from jax import lax
from jax.experimental import pallas as pl
from jax.experimental.pallas import tpu as pltpu
from jax.sharding import PartitionSpec as P

HEADS = 16
HEAD_DIM = 128
TILE = 128
TILES = 128
SLICES = 8
PAIRS = TILE // SLICES // 2
MSG = 2 * PAIRS + 1
STEP_HEADS = 4
STEPS = HEADS // STEP_HEADS
STEP_COLS = STEP_HEADS * HEAD_DIM
EPSILON = 1e-06
SCALE = 4.0 / HEAD_DIM
SCALE_LOG2 = SCALE * math.log2(math.e)
F32 = jnp.float32
BF16 = jnp.bfloat16
GROUP = 8
VMEM_LIMIT = 16 * 1024 * 1024


def dot_nt(a, b):
    return lax.dot_general(a, b, (((1,), (1,)), ((), ())), preferred_element_type=F32)


def dot_nn(a, b):
    return lax.dot_general(a, b, (((1,), (0,)), ((), ())), preferred_element_type=F32)


def dot_tn(a, b):
    return lax.dot_general(a, b, (((0,), (0,)), ((), ())), preferred_element_type=F32)


def split_pair(x):
    high = x.astype(BF16).astype(F32)
    return high, x - high


def normalise(raw):
    factor = lax.rsqrt(jnp.mean(raw * raw, axis=-1, keepdims=True) + EPSILON)
    return factor, (raw * factor).astype(BF16)


def head_columns(j):
    return slice(j * HEAD_DIM, (j + 1) * HEAD_DIM)


def grid_of(axis):
    return lax.broadcasted_iota(jnp.int32, (TILE, TILE), axis)


def pick(upper, if_upper, if_lower):
    return jnp.where(upper, if_upper.astype(F32), if_lower.astype(F32)).astype(BF16)


def in_step(heads):
    while heads:
        heads = [head for head in heads if next(head, head) is not head]


def pack_kernel(
    me_ref, route_hbm, qk_hbm, v_hbm, g_hbm, o_ref, upper_ref, partner_ref, route_buf, *scratch
):
    buffers, sems = scratch[:3], scratch[3]
    inputs = (qk_hbm, v_hbm, g_hbm)

    def loads(step):
        span = pl.ds(step * STEP_COLS, STEP_COLS)
        return [
            pltpu.make_async_copy(hbm.at[:, span], buf.at[:, span], sems.at[step, k])
            for k, (hbm, buf) in enumerate(zip(inputs, buffers))
        ]

    route_load = pltpu.make_async_copy(route_hbm, route_buf, sems.at[STEPS, 0])
    route_load.start()
    for step in range(STEPS):
        for load in loads(step):
            load.start()
    qk_buf, v_buf, g_buf = buffers

    route_load.wait()
    me = me_ref[0]
    route = route_buf[...]
    tiles = lax.broadcasted_iota(jnp.int32, route.shape, 1)
    own = jnp.sum(jnp.where(tiles == me, route, 0), axis=1, keepdims=True)
    earlier = jnp.where((route == own) & (tiles < me), 1.0, 0.0)
    uppers = jnp.max(earlier, axis=1, keepdims=True)
    upper_ref[...] = uppers.astype(jnp.int32)
    heads = lax.broadcasted_iota(jnp.int32, route.shape, 0)
    labels = jnp.sum(jnp.where(heads == me // SLICES, route, 0), axis=0, keepdims=True)
    labels = jnp.broadcast_to(labels, (TILES, TILES))
    diagonal = grid_of(0) == grid_of(1)
    column = jnp.sum(jnp.where(diagonal, labels, 0), axis=1, keepdims=True)
    same = (labels == column) & jnp.logical_not(diagonal)
    partner_ref[...] = jnp.sum(jnp.where(same, grid_of(0), 0), axis=0, keepdims=True)
    at_most = grid_of(0) <= grid_of(1)

    def head(j):
        upper = uppers[j : j + 1, :] > 0.0
        value = v_buf[:, head_columns(j)]
        grad = g_buf[:, head_columns(j)]
        _, normed = normalise(qk_buf[:, head_columns(j)].astype(F32))
        second = pick(upper, grad, value)
        o_ref[j, :, 0:PAIRS] = normed.reshape(SLICES, PAIRS, 2, HEAD_DIM)
        o_ref[j, :, PAIRS : 2 * PAIRS] = second.reshape(SLICES, PAIRS, 2, HEAD_DIM)
        yield
        weights = jnp.where(at_most, jnp.exp2(dot_nt(normed, normed) * SCALE_LOG2), 0.0)
        grad_probs = dot_nt(value, grad)
        yield
        total = jnp.sum(weights, axis=0, keepdims=True)
        moment = jnp.sum(weights * grad_probs, axis=0, keepdims=True)
        yield
        stats = jnp.concatenate(
            [*split_pair(total), *split_pair(moment), jnp.zeros((12, TILE), F32)], axis=0
        ).astype(BF16)
        o_ref[j, :, 2 * PAIRS] = stats.reshape(SLICES, 2, TILE)

    for step in range(STEPS):
        for load in loads(step):
            load.wait()
        in_step([head(step * STEP_HEADS + j) for j in range(STEP_HEADS)])


def pack(me, route, qk, value, grad):
    shape = (HEADS, SLICES, MSG, 2, HEAD_DIM)
    buffer = pltpu.VMEM((TILE, HEADS * HEAD_DIM), BF16)
    hbm = pl.BlockSpec(memory_space=pltpu.HBM)
    return pl.pallas_call(
        pack_kernel,
        out_shape=(
            jax.ShapeDtypeStruct(shape, BF16),
            jax.ShapeDtypeStruct((HEADS, 1), jnp.int32),
            jax.ShapeDtypeStruct((1, TILES), jnp.int32),
        ),
        in_specs=[pl.BlockSpec(memory_space=pltpu.SMEM), hbm, hbm, hbm, hbm],
        out_specs=(pl.BlockSpec(memory_space=pltpu.VMEM),) * 3,
        scratch_shapes=[
            pltpu.VMEM((HEADS, TILES), jnp.int32),
            buffer,
            buffer,
            buffer,
            pltpu.SemaphoreType.DMA((STEPS + 1, 3)),
        ],
        compiler_params=pltpu.CompilerParams(vmem_limit_bytes=VMEM_LIMIT),
        name="pack",
    )(me, *[pltpu.with_memory_space_constraint(x, pltpu.HBM) for x in (route, qk, value, grad)])


def swap_kernel(partner_ref, x_ref, o_ref):
    def move(t, carry):
        o_ref[t] = x_ref[partner_ref[0, t]]
        return carry

    lax.fori_loop(0, TILES, move, 0, unroll=16)


def swap(partner, x):
    whole = pl.BlockSpec(memory_space=pltpu.VMEM)
    return pl.pallas_call(
        swap_kernel,
        out_shape=jax.ShapeDtypeStruct(x.shape, x.dtype),
        in_specs=[pl.BlockSpec(memory_space=pltpu.SMEM), whole],
        out_specs=whole,
        compiler_params=pltpu.CompilerParams(vmem_limit_bytes=VMEM_LIMIT),
        name="swap",
    )(partner, x)


def finish_kernel(
    upper_ref, qk_ref, v_ref, g_ref, z_ref, out_hbm, dqk_ref, dv_ref, out_buf, sems
):
    def store(step):
        span = pl.ds(step * STEP_COLS, STEP_COLS)
        return pltpu.make_async_copy(out_buf.at[:, span], out_hbm.at[:, span], sems.at[step])

    ahead = grid_of(0) - grid_of(1)

    def head(j):
        upper = upper_ref[j, 0] != 0
        value = v_ref[:, head_columns(j)]
        grad = g_ref[:, head_columns(j)]
        raw = qk_ref[:, head_columns(j)].astype(F32)
        factor, normed = normalise(raw)
        second = pick(upper, grad, value)
        first = pick(upper, value, grad)
        their_normed = z_ref[j, :, 0:PAIRS].reshape(TILE, HEAD_DIM)
        their_second = z_ref[j, :, PAIRS : 2 * PAIRS].reshape(TILE, HEAD_DIM)
        stats = z_ref[j, :, 2 * PAIRS].reshape(2 * SLICES, TILE).astype(F32)
        their_total = stats[0:1] + stats[1:2]
        their_moment = stats[2:3] + stats[3:4]
        keys = jnp.concatenate([normed, their_normed], axis=0)
        others = jnp.concatenate([first, their_second], axis=0)
        yield
        weights = jnp.exp2(dot_nt(normed, keys) * SCALE_LOG2)
        grad_probs = dot_nt(second, others)
        yield
        inside = jnp.where(upper, ahead, -ahead) >= 0
        own_w = jnp.where(inside, weights[:, :TILE], 0.0)
        cross_w = weights[:, TILE:]
        own_g = grad_probs[:, :TILE]
        cross_g = grad_probs[:, TILE:]
        inv_row = 1.0 / jnp.sum(own_w + cross_w, axis=1, keepdims=True)
        own_inv = 1.0 / jnp.sum(own_w, axis=0, keepdims=True)
        cross_inv = 1.0 / (their_total + jnp.sum(cross_w, axis=0, keepdims=True))
        yield
        own_p = (own_w * jnp.where(upper, inv_row, own_inv)).astype(BF16)
        cross_p = (cross_w * jnp.where(upper, inv_row, cross_inv)).astype(BF16)
        own_f = own_p.astype(F32)
        cross_f = cross_p.astype(F32)
        own_t = own_f * own_g
        cross_t = cross_f * cross_g
        yield
        row_sum = jnp.sum(own_t + cross_t, axis=1, keepdims=True)
        own_sum = jnp.sum(own_t, axis=0, keepdims=True)
        cross_sum = their_moment * cross_inv + jnp.sum(cross_t, axis=0, keepdims=True)
        yield
        own_s = own_f * (own_g - jnp.where(upper, row_sum, own_sum))
        cross_s = cross_f * (cross_g - jnp.where(upper, row_sum, cross_sum))
        own_s = own_s.astype(BF16)
        scores = jnp.concatenate([own_s, cross_s.astype(BF16)], axis=1)
        along = dot_nn(jnp.concatenate([own_p, cross_p], axis=1), others)
        across = dot_tn(own_p, second)
        grad_normed = dot_nn(scores, keys) + dot_tn(own_s, normed)
        yield
        out_buf[:, head_columns(j)] = jnp.where(upper, along, across).astype(BF16)
        dv_ref[:, head_columns(j)] = jnp.where(upper, across, along).astype(BF16)
        grad_normed = (grad_normed * SCALE).astype(BF16).astype(F32)
        inner = jnp.mean(raw * grad_normed, axis=-1, keepdims=True)
        grad_input = factor * grad_normed - raw * (factor**3 * inner)
        dqk_ref[:, head_columns(j)] = grad_input.astype(BF16)

    for start in range(0, HEADS, GROUP):
        in_step([head(start + j) for j in range(GROUP)])
        for step in range(start // STEP_HEADS, (start + GROUP) // STEP_HEADS):
            store(step).start()
    for step in range(STEPS):
        store(step).wait()


def finish(upper, qk, value, grad, z):
    shape = jax.ShapeDtypeStruct((TILE, HEADS * HEAD_DIM), BF16)
    whole = pl.BlockSpec(memory_space=pltpu.VMEM)
    return pl.pallas_call(
        finish_kernel,
        out_shape=(pltpu.HBM(shape.shape, shape.dtype), shape, shape),
        in_specs=[pl.BlockSpec(memory_space=pltpu.SMEM)] + [whole] * 4,
        out_specs=(pl.BlockSpec(memory_space=pltpu.HBM), whole, whole),
        scratch_shapes=[pltpu.VMEM(shape.shape, BF16), pltpu.SemaphoreType.DMA((STEPS,))],
        compiler_params=pltpu.CompilerParams(vmem_limit_bytes=VMEM_LIMIT),
        name="finish",
    )(upper, qk, value, grad, z)


def deliver_kernel(a_ref, b_ref, a_hbm, b_hbm, sems):
    copies = [
        pltpu.make_async_copy(a_ref, a_hbm, sems.at[0]),
        pltpu.make_async_copy(b_ref, b_hbm, sems.at[1]),
    ]
    for copy in copies:
        copy.start()
    for copy in copies:
        copy.wait()


def deliver(a, b):
    whole = pl.BlockSpec(memory_space=pltpu.VMEM)
    hbm = pl.BlockSpec(memory_space=pltpu.HBM)
    return pl.pallas_call(
        deliver_kernel,
        out_shape=(pltpu.HBM(a.shape, a.dtype), pltpu.HBM(b.shape, b.dtype)),
        in_specs=[whole, whole],
        out_specs=(hbm, hbm),
        scratch_shapes=[pltpu.SemaphoreType.DMA((2,))],
        compiler_params=pltpu.CompilerParams(vmem_limit_bytes=VMEM_LIMIT),
        name="deliver",
    )(a, b)


def exchange(x):
    return lax.all_to_all(x, "seq", split_axis=0, concat_axis=0, tiled=True)


def local(query_key, payload_matrix, out_grad, route_assignment):
    me = lax.axis_index("seq")
    route = route_assignment[0]
    rows = (query_key[0], payload_matrix[0], out_grad[0])
    packed, upper, partner = pack(me.reshape(1), route.T, *rows)
    slices = exchange(packed.reshape(TILES, MSG, 2, HEAD_DIM))
    theirs = exchange(swap(partner, slices)).reshape(HEADS, SLICES, MSG, 2, HEAD_DIM)
    out, grad_qk, grad_v = finish(upper, *rows, theirs)
    grad_qk, grad_v = deliver(*lax.ppermute((grad_qk, grad_v), "pipe", [(0, 1), (1, 0)]))
    return (out[None], grad_qk[None], grad_v[None])


def solution(mesh):
    rows = P("pipe", "seq", None)
    return jax.shard_map(
        local,
        mesh=mesh,
        in_specs=(rows, rows, rows, P("pipe", None, None)),
        out_specs=(rows, rows, rows),
        check_vma=False,
    )
```

time: 102 us -> 99 us (0.971)
  blocking collectives: 0 us -> 81.5 us
  waiting for transfers between devices: 57.8 us -> 2.19 us
  starting transfers between devices: 30.7 us -> 4.89 us
  local copies, waits for them, and re-layouts: 1.81 us -> 0.02 us
    all_to_all x0 -> x2, blocking collectives: none -> 81.5 us  [exchange(): return lax.all_to_all(x, 'seq', split_axis=0, concat_axis=0, tiled=True)]
    all_to_all x2 -> x0, waiting for transfers between devices: 55.6 us -> none  [exchange(): return lax.all_to_all(x, 'seq', split_axis=0, concat_axis=0, tiled=True)]
    all_to_all x2 -> x0, starting transfers between devices: 25.8 us -> none  [exchange(): return lax.all_to_all(x, 'seq', split_axis=0, concat_axis=0, tiled=True)]
    unnamed x10 -> x6, local copies, waits for them, and re-layouts: 1.61 us -> 0.02 us
  transfers between devices with their start and end apart: 4 -> 2, of which waited for: 4 -> 2; matrix products, arithmetic and copies ran while one was open for 0% -> 0% of each run, Pallas kernels for 0% -> 0%
where the time goes in v3:
time: 99 us; the launch traced here: 98.8 us
  blocking collectives  81.5 us (82%)
  Pallas kernels  9.51 us (10%)
  starting transfers between devices  4.89 us (5%)
  waiting for transfers between devices  2.19 us (2%)
    all_to_all x2, blocking collectives, exchange(): return lax.all_to_all(x, 'seq', split_axis=0, concat_axis=0, tiled=True)  81.5 us
    ppermute x2, starting transfers between devices, local(): lax.ppermute((grad_qk, grad_v), 'pipe', [(0, 1), (1, 0)])  4.89 us
    pallas_call x1, Pallas kernels, finish(): pl.pallas_call(finish_kernel, out_shape=(pltpu.HBM(shape.shape, shape.dty...  4.83 us
    pallas_call x1, Pallas kernels, pack(): pl.pallas_call(pack_kernel, out_shape=(jax.ShapeDtypeStruct(shape, BF16),...  2.96 us
    ppermute x2, waiting for transfers between devices, local(): lax.ppermute((grad_qk, grad_v), 'pipe', [(0, 1), (1, 0)])  2.19 us
  transfers between devices with their start and end apart: 2, of which 2 were waited for; matrix products, arithmetic and copies ran while one was open for 0% of the time, Pallas kernels for 0%

profile of v3, /device:TPU:1, one launch (start us, length us, event | category | flops | bytes accessed | tf_op | source)
XLA Modules:
  0.0 98.8 jit_solution(4760689177757304189)
XLA Ops:
  0.6 3.0 %pack.1 = (bf16[16,8,17,2,128]{4,3,2,1,0:T(2,128)(2,1)S(1)}, s32[16,1]{1,0:T(8,128)S(1)}, s32[1,128]{1,0:T(1,128)S(1)}) custom-call(s32[1]{0:T(128)} %bitcast.me_ref, s32[16,128]{1,0:T(8,128)} %bitcast.20, bf16[128,2048]{1,0:T(8,128)(2,1)} %bitcast.13, bf16[128,2048]{1,0:T(8,128)(2,1)} %bitcast.15, bf16[128,2048]{1,0:T(8,128)(2,1)} %bitcast.17), custom_call_target="tpu_custom_call" | custom-call | tf_op jit(solution)/shard_map/pack/pallas_call | solution.py:135
  3.6 44.7 %all_to_all.10.x_ref = bf16[128,17,2,128]{3,2,1,0:T(2,128)(2,1)S(1)} all-to-all(bf16[128,17,2,128]{3,2,1,0:T(2,128)(2,1)S(1)} %bitcast.19), channel_id=1, replica_groups=mesh['seq'=128,'pipe'=2] {'seq'}, dimensions={0} | all-to-all | bytes 2228224 | tf_op jit(solution)/shard_map/all_to_all | solution.py:287
  48.3 0.7 swap.1
  49.0 0.0 copy-start
  49.0 0.0 copy-start.1
  49.0 0.0 copy-start.2
  49.0 36.8 %all_to_all.11 = bf16[128,17,2,128]{3,2,1,0:T(2,128)(2,1)S(1)} all-to-all(bf16[128,17,2,128]{3,2,1,0:T(2,128)(2,1)S(1)} %swap.1), channel_id=1, replica_groups=mesh['seq'=128,'pipe'=2] {'seq'}, dimensions={0} | all-to-all | bytes 2228224 | tf_op jit(solution)/shard_map/all_to_all | solution.py:287
  85.9 0.0 copy-done
  85.9 0.0 copy-done.1
  85.9 0.0 copy-done.2
  85.9 4.8 %finish.1 = (bf16[128,2048]{1,0:T(8,128)(2,1)}, bf16[128,2048]{1,0:T(8,128)(2,1)S(1)}, bf16[128,2048]{1,0:T(8,128)(2,1)S(1)}) custom-call(s32[16,1]{1,0:T(8,128)S(1)} %get-tuple-element.11.upper_ref, bf16[128,2048]{1,0:T(8,128)(2,1)S(1)} %bitcast.14, bf16[128,2048]{1,0:T(8,128)(2,1)S(1)} %bitcast.16, bf16[128,2048]{1,0:T(8,128)(2,1)S(1)} %bitcast.18, ...), custom_call_target="tpu_custom_call" | custom-call | tf_op jit(solution)/shard_map/finish/pallas_call | solution.py:250
  90.7 4.8 %collective-permute-start = (bf16[128,2048]{1,0:T(8,128)(2,1)S(1)}, bf16[128,2048]{1,0:T(8,128)(2,1)S(1)}, u32[]{:S(2)}, u32[]{:S(2)}) collective-permute-start(bf16[128,2048]{1,0:T(8,128)(2,1)S(1)} %get-tuple-element.15), channel_id=1, source_target_pairs={{0,1},{1,0},{2,3},{3,2},{4,5},{5,4},{6,7},{7,6},{8,9},{9,8},{10,11... | collective-permute-start | bytes 1572872 | tf_op jit(solution)/shard_map/ppermute | solution.py:298
  95.5 0.1 collective-permute-start.1
  95.6 1.4 %collective-permute-done.a_ref = bf16[128,2048]{1,0:T(8,128)(2,1)S(1)} collective-permute-done((bf16[128,2048]{1,0:T(8,128)(2,1)S(1)}, bf16[128,2048]{1,0:T(8,128)(2,1)S(1)}, u32[]{:S(2)}, u32[]{:S(2)}) %collective-permute-start) | collective-permute-done | bytes 524320 | tf_op jit(solution)/shard_map/ppermute | solution.py:298
  97.1 0.7 collective-permute-done.1.b_ref
  97.8 1.0 deliver.1
Async XLA Ops:
  49.0 36.9 %copy-start = (bf16[1,128,2048]{2,1,0:T(8,128)(2,1)S(1)}, bf16[1,128,2048]{2,1,0:T(8,128)(2,1)}, u32[]{:S(2)}) copy-start(bf16[1,128,2048]{2,1,0:T(8,128)(2,1)} %param.4) | copy-start | bytes 1572868
  49.0 36.9 %copy-start.1 = (bf16[1,128,2048]{2,1,0:T(8,128)(2,1)S(1)}, bf16[1,128,2048]{2,1,0:T(8,128)(2,1)}, u32[]{:S(2)}) copy-start(bf16[1,128,2048]{2,1,0:T(8,128)(2,1)} %param.5) | copy-start | bytes 1572868
  49.0 36.9 %copy-start.2 = (bf16[1,128,2048]{2,1,0:T(8,128)(2,1)S(1)}, bf16[1,128,2048]{2,1,0:T(8,128)(2,1)}, u32[]{:S(2)}) copy-start(bf16[1,128,2048]{2,1,0:T(8,128)(2,1)} %param.6) | copy-start | bytes 1572868
  90.7 6.3 %collective-permute-start = (bf16[128,2048]{1,0:T(8,128)(2,1)S(1)}, bf16[128,2048]{1,0:T(8,128)(2,1)S(1)}, u32[]{:S(2)}, u32[]{:S(2)}) collective-permute-start(bf16[128,2048]{1,0:T(8,128)(2,1)S(1)} %get-tuple-element.15), channel_id=1, source_target_pairs={{0,1},{1,0},{2,3},{3,2},{4,5},{5,4},{6,7},{7,6},{8,9},{9,8},{10,11... | collective-permute-start | bytes 1572872 | tf_op jit(solution)/shard_map/ppermute | solution.py:298
  95.5 2.3 %collective-permute-start.1 = (bf16[128,2048]{1,0:T(8,128)(2,1)S(1)}, bf16[128,2048]{1,0:T(8,128)(2,1)S(1)}, u32[]{:S(2)}, u32[]{:S(2)}) collective-permute-start(bf16[128,2048]{1,0:T(8,128)(2,1)S(1)} %get-tuple-element.16), channel_id=1, source_target_pairs={{0,1},{1,0},{2,3},{3,2},{4,5},{5,4},{6,7},{7,6},{8,9},{9,8},{10,11... | collective-permute-start | bytes 1572872 | tf_op jit(solution)/shard_map/ppermute | solution.py:298

commit v4 on v3

--- a/solution.py
+++ b/solution.py
@@ -57,7 +57,7 @@
 
 
 def pick(upper, if_upper, if_lower):
-    return jnp.where(upper, if_upper.astype(F32), if_lower.astype(F32)).astype(BF16)
+    return jnp.where(upper, if_upper, if_lower)
 
 
 def in_step(heads):
@@ -66,7 +66,7 @@
 
 
 def pack_kernel(
-    me_ref, route_hbm, qk_hbm, v_hbm, g_hbm, o_ref, upper_ref, partner_ref, route_buf, *scratch
+    route_hbm, qk_hbm, v_hbm, g_hbm, o_ref, upper_ref, partner_ref, route_buf, *scratch
 ):
     buffers, sems = scratch[:3], scratch[3]
     inputs = (qk_hbm, v_hbm, g_hbm)
@@ -86,7 +86,7 @@
     qk_buf, v_buf, g_buf = buffers
 
     route_load.wait()
-    me = me_ref[0]
+    me = lax.axis_index("seq")
     route = route_buf[...]
     tiles = lax.broadcasted_iota(jnp.int32, route.shape, 1)
     own = jnp.sum(jnp.where(tiles == me, route, 0), axis=1, keepdims=True)
@@ -128,7 +128,7 @@
         in_step([head(step * STEP_HEADS + j) for j in range(STEP_HEADS)])
 
 
-def pack(me, route, qk, value, grad):
+def pack(route, qk, value, grad):
     shape = (HEADS, SLICES, MSG, 2, HEAD_DIM)
     buffer = pltpu.VMEM((TILE, HEADS * HEAD_DIM), BF16)
     hbm = pl.BlockSpec(memory_space=pltpu.HBM)
@@ -139,7 +139,7 @@
             jax.ShapeDtypeStruct((HEADS, 1), jnp.int32),
             jax.ShapeDtypeStruct((1, TILES), jnp.int32),
         ),
-        in_specs=[pl.BlockSpec(memory_space=pltpu.SMEM), hbm, hbm, hbm, hbm],
+        in_specs=[hbm, hbm, hbm, hbm],
         out_specs=(pl.BlockSpec(memory_space=pltpu.VMEM),) * 3,
         scratch_shapes=[
             pltpu.VMEM((HEADS, TILES), jnp.int32),
@@ -150,7 +150,7 @@
         ],
         compiler_params=pltpu.CompilerParams(vmem_limit_bytes=VMEM_LIMIT),
         name="pack",
-    )(me, *[pltpu.with_memory_space_constraint(x, pltpu.HBM) for x in (route, qk, value, grad)])
+    )(*[pltpu.with_memory_space_constraint(x, pltpu.HBM) for x in (route, qk, value, grad)])
 
 
 def swap_kernel(partner_ref, x_ref, o_ref):
@@ -173,17 +173,12 @@
     )(partner, x)
 
 
-def finish_kernel(
-    upper_ref, qk_ref, v_ref, g_ref, z_ref, out_hbm, dqk_ref, dv_ref, out_buf, sems
-):
-    def store(step):
-        span = pl.ds(step * STEP_COLS, STEP_COLS)
-        return pltpu.make_async_copy(out_buf.at[:, span], out_hbm.at[:, span], sems.at[step])
-
+def finish_kernel(upper_ref, qk_ref, v_ref, g_ref, z_ref, out_ref, dqk_ref, dv_ref):
+    uppers = upper_ref[...]
     ahead = grid_of(0) - grid_of(1)
 
     def head(j):
-        upper = upper_ref[j, 0] != 0
+        upper = uppers[j : j + 1, :] != 0
         value = v_ref[:, head_columns(j)]
         grad = g_ref[:, head_columns(j)]
         raw = qk_ref[:, head_columns(j)].astype(F32)
@@ -229,7 +224,7 @@
         across = dot_tn(own_p, second)
         grad_normed = dot_nn(scores, keys) + dot_tn(own_s, normed)
         yield
-        out_buf[:, head_columns(j)] = jnp.where(upper, along, across).astype(BF16)
+        out_ref[:, head_columns(j)] = jnp.where(upper, along, across).astype(BF16)
         dv_ref[:, head_columns(j)] = jnp.where(upper, across, along).astype(BF16)
         grad_normed = (grad_normed * SCALE).astype(BF16).astype(F32)
         inner = jnp.mean(raw * grad_normed, axis=-1, keepdims=True)
@@ -238,10 +233,6 @@
 
     for start in range(0, HEADS, GROUP):
         in_step([head(start + j) for j in range(GROUP)])
-        for step in range(start // STEP_HEADS, (start + GROUP) // STEP_HEADS):
-            store(step).start()
-    for step in range(STEPS):
-        store(step).wait()
 
 
 def finish(upper, qk, value, grad, z):
@@ -249,38 +240,33 @@
     whole = pl.BlockSpec(memory_space=pltpu.VMEM)
     return pl.pallas_call(
         finish_kernel,
-        out_shape=(pltpu.HBM(shape.shape, shape.dtype), shape, shape),
-        in_specs=[pl.BlockSpec(memory_space=pltpu.SMEM)] + [whole] * 4,
-        out_specs=(pl.BlockSpec(memory_space=pltpu.HBM), whole, whole),
-        scratch_shapes=[pltpu.VMEM(shape.shape, BF16), pltpu.SemaphoreType.DMA((STEPS,))],
+        out_shape=(shape, shape, shape),
+        in_specs=[whole] * 5,
+        out_specs=(whole, whole, whole),
         compiler_params=pltpu.CompilerParams(vmem_limit_bytes=VMEM_LIMIT),
         name="finish",
     )(upper, qk, value, grad, z)
 
 
-def deliver_kernel(a_ref, b_ref, a_hbm, b_hbm, sems):
-    copies = [
-        pltpu.make_async_copy(a_ref, a_hbm, sems.at[0]),
-        pltpu.make_async_copy(b_ref, b_hbm, sems.at[1]),
-    ]
-    for copy in copies:
-        copy.start()
-    for copy in copies:
-        copy.wait()
-
-
-def deliver(a, b):
-    whole = pl.BlockSpec(memory_space=pltpu.VMEM)
-    hbm = pl.BlockSpec(memory_space=pltpu.HBM)
+def deliver_kernel(x_ref, o_hbm, sem):
+    copy = pltpu.make_async_copy(x_ref, o_hbm, sem)
+    copy.start()
+    copy.wait()
+
+
+def deliver(x):
     return pl.pallas_call(
         deliver_kernel,
-        out_shape=(pltpu.HBM(a.shape, a.dtype), pltpu.HBM(b.shape, b.dtype)),
-        in_specs=[whole, whole],
-        out_specs=(hbm, hbm),
-        scratch_shapes=[pltpu.SemaphoreType.DMA((2,))],
-        compiler_params=pltpu.CompilerParams(vmem_limit_bytes=VMEM_LIMIT),
+        out_shape=pltpu.HBM(x.shape, x.dtype),
+        in_specs=[pl.BlockSpec(memory_space=pltpu.VMEM)],
+        out_specs=pl.BlockSpec(memory_space=pltpu.HBM),
+        scratch_shapes=[pltpu.SemaphoreType.DMA],
+        compiler_params=pltpu.CompilerParams(vmem_limit_bytes=VMEM_LIMIT),
+        cost_estimate=pl.CostEstimate(
+            flops=0, bytes_accessed=2 * x.size * x.dtype.itemsize, transcendentals=0
+        ),
         name="deliver",
-    )(a, b)
+    )(x)
 
 
 def exchange(x):
@@ -288,14 +274,14 @@
 
 
 def local(query_key, payload_matrix, out_grad, route_assignment):
-    me = lax.axis_index("seq")
     route = route_assignment[0]
     rows = (query_key[0], payload_matrix[0], out_grad[0])
-    packed, upper, partner = pack(me.reshape(1), route.T, *rows)
+    packed, upper, partner = pack(route.T, *rows)
     slices = exchange(packed.reshape(TILES, MSG, 2, HEAD_DIM))
     theirs = exchange(swap(partner, slices)).reshape(HEADS, SLICES, MSG, 2, HEAD_DIM)
     out, grad_qk, grad_v = finish(upper, *rows, theirs)
-    grad_qk, grad_v = deliver(*lax.ppermute((grad_qk, grad_v), "pipe", [(0, 1), (1, 0)]))
+    grad_qk, grad_v = lax.ppermute((grad_qk, grad_v), "pipe", [(0, 1), (1, 0)])
+    out, grad_qk, grad_v = deliver(out), deliver(grad_qk), deliver(grad_v)
     return (out[None], grad_qk[None], grad_v[None])
 
 

time: 99 us -> 97.5 us (0.985)
  waiting for transfers between devices: 2.19 us -> 0.63 us
    ppermute x2, waiting for transfers between devices: 2.19 us -> 0.63 us  [local(): grad_qk, grad_v = lax.ppermute((grad_qk, grad_v), 'pipe', [(0, 1), (1, 0)])]
    pallas_call x2 -> x4, Pallas kernels: 5.81 us -> 5.9 us  [the longest x1 3.49 us: finish(): pl.pallas_call(finish_kernel, out_shape=(shape, shape, shape), in_specs=[...]
  transfers between devices with their start and end apart: 2 -> 2, of which waited for: 2 -> 1; matrix products, arithmetic and copies ran while one was open for 0% -> 0% of each run, Pallas kernels for 0% -> 2%
where the time goes in v4:
time: 97.5 us; the launch traced here: 97.3 us
  blocking collectives  81.5 us (84%)
  Pallas kernels  9.55 us (10%)
  starting transfers between devices  4.89 us (5%)
    all_to_all x2, blocking collectives, exchange(): return lax.all_to_all(x, 'seq', split_axis=0, concat_axis=0, tiled=True)  81.5 us
    ppermute x2, starting transfers between devices, local(): grad_qk, grad_v = lax.ppermute((grad_qk, grad_v), 'pipe', [(0, 1), (1, 0)])  4.89 us
    pallas_call x1, Pallas kernels, finish(): pl.pallas_call(finish_kernel, out_shape=(shape, shape, shape), in_specs=[...  3.49 us
    pallas_call x1, Pallas kernels, pack(): pl.pallas_call(pack_kernel, out_shape=(jax.ShapeDtypeStruct(shape, BF16),...  2.92 us
    pallas_call x3, Pallas kernels, deliver(): pl.pallas_call(deliver_kernel, out_shape=pltpu.HBM(x.shape, x.dtype), in_...  2.4 us
  transfers between devices with their start and end apart: 2, of which 1 were waited for; matrix products, arithmetic and copies ran while one was open for 0% of the time, Pallas kernels for 2%

profile of v4, /device:TPU:1, one launch (start us, length us, event | category | flops | bytes accessed | tf_op | source)
XLA Modules:
  0.0 97.3 jit_solution(6558049480415130656)
XLA Ops:
  0.6 2.9 %pack.1 = (bf16[16,8,17,2,128]{4,3,2,1,0:T(2,128)(2,1)S(1)}, s32[16,1]{1,0:T(8,128)S(1)}, s32[1,128]{1,0:T(1,128)S(1)}) custom-call(s32[16,128]{1,0:T(8,128)} %bitcast.22, bf16[128,2048]{1,0:T(8,128)(2,1)} %bitcast.12, bf16[128,2048]{1,0:T(8,128)(2,1)} %bitcast.14, bf16[128,2048]{1,0:T(8,128)(2,1)} %bitcast.16), custom_call_target="tpu_custom_call" | custom-call | tf_op jit(solution)/shard_map/pack/pallas_call | solution.py:135
  3.6 44.7 %all_to_all.10.x_ref = bf16[128,17,2,128]{3,2,1,0:T(2,128)(2,1)S(1)} all-to-all(bf16[128,17,2,128]{3,2,1,0:T(2,128)(2,1)S(1)} %bitcast.18), channel_id=1, replica_groups=mesh['seq'=128,'pipe'=2] {'seq'}, dimensions={0} | all-to-all | bytes 2228224 | tf_op jit(solution)/shard_map/all_to_all | solution.py:273
  48.2 0.7 swap.1
  49.0 0.0 copy-start
  49.0 0.0 copy-start.1
  49.0 0.0 copy-start.2
  49.0 36.8 %all_to_all.11 = bf16[128,17,2,128]{3,2,1,0:T(2,128)(2,1)S(1)} all-to-all(bf16[128,17,2,128]{3,2,1,0:T(2,128)(2,1)S(1)} %swap.1), channel_id=1, replica_groups=mesh['seq'=128,'pipe'=2] {'seq'}, dimensions={0} | all-to-all | bytes 2228224 | tf_op jit(solution)/shard_map/all_to_all | solution.py:273
  85.8 0.0 copy-done
  85.8 0.0 copy-done.1
  85.8 0.0 copy-done.2
  85.9 3.5 %finish.1 = (bf16[128,2048]{1,0:T(8,128)(2,1)S(1)}, bf16[128,2048]{1,0:T(8,128)(2,1)S(1)}, bf16[128,2048]{1,0:T(8,128)(2,1)S(1)}) custom-call(s32[16,1]{1,0:T(8,128)S(1)} %get-tuple-element.9.upper_ref, bf16[128,2048]{1,0:T(8,128)(2,1)S(1)} %bitcast.13, bf16[128,2048]{1,0:T(8,128)(2,1)S(1)} %bitcast.15, bf16[128,2048]{1,0:T(8,128)(2,1)S(1)} %bitcast.17, ...), custom_call_target="tpu_custom_call" | custom-call | tf_op jit(solution)/shard_map/finish/pallas_call | solution.py:241
  89.4 4.8 %collective-permute-start = (bf16[128,2048]{1,0:T(8,128)(2,1)S(1)}, bf16[128,2048]{1,0:T(8,128)(2,1)S(1)}, u32[]{:S(2)}, u32[]{:S(2)}) collective-permute-start(bf16[128,2048]{1,0:T(8,128)(2,1)S(1)} %get-tuple-element.13), channel_id=1, source_target_pairs={{0,1},{1,0},{2,3},{3,2},{4,5},{5,4},{6,7},{7,6},{8,9},{9,8},{10,11... | collective-permute-start | bytes 1572872 | tf_op jit(solution)/shard_map/ppermute | solution.py:283
  94.1 0.1 collective-permute-start.1
  94.2 0.8 deliver.3
  95.1 0.6 collective-permute-done.x_ref
  95.7 0.8 deliver.4
  96.5 0.0 collective-permute-done.1.x_ref
  96.5 0.8 deliver.5
Async XLA Ops:
  49.0 36.9 %copy-start = (bf16[1,128,2048]{2,1,0:T(8,128)(2,1)S(1)}, bf16[1,128,2048]{2,1,0:T(8,128)(2,1)}, u32[]{:S(2)}) copy-start(bf16[1,128,2048]{2,1,0:T(8,128)(2,1)} %param.4) | copy-start | bytes 1572868
  49.0 36.9 %copy-start.1 = (bf16[1,128,2048]{2,1,0:T(8,128)(2,1)S(1)}, bf16[1,128,2048]{2,1,0:T(8,128)(2,1)}, u32[]{:S(2)}) copy-start(bf16[1,128,2048]{2,1,0:T(8,128)(2,1)} %param.5) | copy-start | bytes 1572868
  49.0 36.9 %copy-start.2 = (bf16[1,128,2048]{2,1,0:T(8,128)(2,1)S(1)}, bf16[1,128,2048]{2,1,0:T(8,128)(2,1)}, u32[]{:S(2)}) copy-start(bf16[1,128,2048]{2,1,0:T(8,128)(2,1)} %param.6) | copy-start | bytes 1572868
  89.4 6.3 %collective-permute-start = (bf16[128,2048]{1,0:T(8,128)(2,1)S(1)}, bf16[128,2048]{1,0:T(8,128)(2,1)S(1)}, u32[]{:S(2)}, u32[]{:S(2)}) collective-permute-start(bf16[128,2048]{1,0:T(8,128)(2,1)S(1)} %get-tuple-element.13), channel_id=1, source_target_pairs={{0,1},{1,0},{2,3},{3,2},{4,5},{5,4},{6,7},{7,6},{8,9},{9,8},{10,11... | collective-permute-start | bytes 1572872 | tf_op jit(solution)/shard_map/ppermute | solution.py:283
  94.1 2.3 %collective-permute-start.1 = (bf16[128,2048]{1,0:T(8,128)(2,1)S(1)}, bf16[128,2048]{1,0:T(8,128)(2,1)S(1)}, u32[]{:S(2)}, u32[]{:S(2)}) collective-permute-start(bf16[128,2048]{1,0:T(8,128)(2,1)S(1)} %get-tuple-element.14), channel_id=1, source_target_pairs={{0,1},{1,0},{2,3},{3,2},{4,5},{5,4},{6,7},{7,6},{8,9},{9,8},{10,11... | collective-permute-start | bytes 1572872 | tf_op jit(solution)/shard_map/ppermute | solution.py:283

commit v5 on v4

--- a/solution.py
+++ b/solution.py
@@ -14,7 +14,7 @@
 SLICES = 8
 PAIRS = TILE // SLICES // 2
 MSG = 2 * PAIRS + 1
-STEP_HEADS = 4
+STEP_HEADS = 8
 STEPS = HEADS // STEP_HEADS
 STEP_COLS = STEP_HEADS * HEAD_DIM
 EPSILON = 1e-06
@@ -193,7 +193,8 @@
         keys = jnp.concatenate([normed, their_normed], axis=0)
         others = jnp.concatenate([first, their_second], axis=0)
         yield
-        weights = jnp.exp2(dot_nt(normed, keys) * SCALE_LOG2)
+        scores = [dot_nt(normed, normed), dot_nt(normed, their_normed)]
+        weights = jnp.exp2(jnp.concatenate(scores, axis=1) * SCALE_LOG2)
         grad_probs = dot_nt(second, others)
         yield
         inside = jnp.where(upper, ahead, -ahead) >= 0

time: 97.5 us -> 97 us (level)
  no operation moved by 1% of the time
where the time goes in v5:
time: 97 us; the launch traced here: 96.8 us
  blocking collectives  81.5 us (84%)
  Pallas kernels  9.07 us (9%)
  starting transfers between devices  4.89 us (5%)
    all_to_all x2, blocking collectives, exchange(): return lax.all_to_all(x, 'seq', split_axis=0, concat_axis=0, tiled=True)  81.5 us
    ppermute x2, starting transfers between devices, local(): grad_qk, grad_v = lax.ppermute((grad_qk, grad_v), 'pipe', [(0, 1), (1, 0)])  4.89 us
    pallas_call x1, Pallas kernels, finish(): pl.pallas_call(finish_kernel, out_shape=(shape, shape, shape), in_specs=[...  3.26 us
    pallas_call x1, Pallas kernels, pack(): pl.pallas_call(pack_kernel, out_shape=(jax.ShapeDtypeStruct(shape, BF16),...  2.67 us
    pallas_call x3, Pallas kernels, deliver(): pl.pallas_call(deliver_kernel, out_shape=pltpu.HBM(x.shape, x.dtype), in_...  2.4 us
  transfers between devices with their start and end apart: 2, of which 1 were waited for; matrix products, arithmetic and copies ran while one was open for 0% of the time, Pallas kernels for 2%

profile of v5, /device:TPU:1, one launch (start us, length us, event | category | flops | bytes accessed | tf_op | source)
XLA Modules:
  0.0 96.8 jit_solution(6692431084380911449)
XLA Ops:
  0.6 2.7 %pack.1 = (bf16[16,8,17,2,128]{4,3,2,1,0:T(2,128)(2,1)S(1)}, s32[16,1]{1,0:T(8,128)S(1)}, s32[1,128]{1,0:T(1,128)S(1)}) custom-call(s32[16,128]{1,0:T(8,128)} %bitcast.22, bf16[128,2048]{1,0:T(8,128)(2,1)} %bitcast.12, bf16[128,2048]{1,0:T(8,128)(2,1)} %bitcast.14, bf16[128,2048]{1,0:T(8,128)(2,1)} %bitcast.16), custom_call_target="tpu_custom_call" | custom-call | tf_op jit(solution)/shard_map/pack/pallas_call | solution.py:135
  3.3 44.7 %all_to_all.10.x_ref = bf16[128,17,2,128]{3,2,1,0:T(2,128)(2,1)S(1)} all-to-all(bf16[128,17,2,128]{3,2,1,0:T(2,128)(2,1)S(1)} %bitcast.18), channel_id=1, replica_groups=mesh['seq'=128,'pipe'=2] {'seq'}, dimensions={0} | all-to-all | bytes 2228224 | tf_op jit(solution)/shard_map/all_to_all | solution.py:274
  48.0 0.7 swap.1
  48.7 0.0 copy-start
  48.7 0.0 copy-start.1
  48.7 0.0 copy-start.2
  48.7 36.8 %all_to_all.11 = bf16[128,17,2,128]{3,2,1,0:T(2,128)(2,1)S(1)} all-to-all(bf16[128,17,2,128]{3,2,1,0:T(2,128)(2,1)S(1)} %swap.1), channel_id=1, replica_groups=mesh['seq'=128,'pipe'=2] {'seq'}, dimensions={0} | all-to-all | bytes 2228224 | tf_op jit(solution)/shard_map/all_to_all | solution.py:274
  85.6 0.0 copy-done
  85.6 0.0 copy-done.1
  85.6 0.0 copy-done.2
  85.6 3.3 %finish.1 = (bf16[128,2048]{1,0:T(8,128)(2,1)S(1)}, bf16[128,2048]{1,0:T(8,128)(2,1)S(1)}, bf16[128,2048]{1,0:T(8,128)(2,1)S(1)}) custom-call(s32[16,1]{1,0:T(8,128)S(1)} %get-tuple-element.9.upper_ref, bf16[128,2048]{1,0:T(8,128)(2,1)S(1)} %bitcast.13, bf16[128,2048]{1,0:T(8,128)(2,1)S(1)} %bitcast.15, bf16[128,2048]{1,0:T(8,128)(2,1)S(1)} %bitcast.17, ...), custom_call_target="tpu_custom_call" | custom-call | tf_op jit(solution)/shard_map/finish/pallas_call | solution.py:242
  88.9 4.8 %collective-permute-start = (bf16[128,2048]{1,0:T(8,128)(2,1)S(1)}, bf16[128,2048]{1,0:T(8,128)(2,1)S(1)}, u32[]{:S(2)}, u32[]{:S(2)}) collective-permute-start(bf16[128,2048]{1,0:T(8,128)(2,1)S(1)} %get-tuple-element.13), channel_id=1, source_target_pairs={{0,1},{1,0},{2,3},{3,2},{4,5},{5,4},{6,7},{7,6},{8,9},{9,8},{10,11... | collective-permute-start | bytes 1572872 | tf_op jit(solution)/shard_map/ppermute | solution.py:284
  93.7 0.1 collective-permute-start.1
  93.8 0.8 deliver.3
  94.6 0.6 collective-permute-done.x_ref
  95.2 0.8 deliver.4
  96.0 0.0 collective-permute-done.1.x_ref
  96.0 0.8 deliver.5
Async XLA Ops:
  48.7 36.9 %copy-start = (bf16[1,128,2048]{2,1,0:T(8,128)(2,1)S(1)}, bf16[1,128,2048]{2,1,0:T(8,128)(2,1)}, u32[]{:S(2)}) copy-start(bf16[1,128,2048]{2,1,0:T(8,128)(2,1)} %param.4) | copy-start | bytes 1572868
  48.7 36.9 %copy-start.1 = (bf16[1,128,2048]{2,1,0:T(8,128)(2,1)S(1)}, bf16[1,128,2048]{2,1,0:T(8,128)(2,1)}, u32[]{:S(2)}) copy-start(bf16[1,128,2048]{2,1,0:T(8,128)(2,1)} %param.5) | copy-start | bytes 1572868
  48.7 36.9 %copy-start.2 = (bf16[1,128,2048]{2,1,0:T(8,128)(2,1)S(1)}, bf16[1,128,2048]{2,1,0:T(8,128)(2,1)}, u32[]{:S(2)}) copy-start(bf16[1,128,2048]{2,1,0:T(8,128)(2,1)} %param.6) | copy-start | bytes 1572868
  88.9 6.3 %collective-permute-start = (bf16[128,2048]{1,0:T(8,128)(2,1)S(1)}, bf16[128,2048]{1,0:T(8,128)(2,1)S(1)}, u32[]{:S(2)}, u32[]{:S(2)}) collective-permute-start(bf16[128,2048]{1,0:T(8,128)(2,1)S(1)} %get-tuple-element.13), channel_id=1, source_target_pairs={{0,1},{1,0},{2,3},{3,2},{4,5},{5,4},{6,7},{7,6},{8,9},{9,8},{10,11... | collective-permute-start | bytes 1572872 | tf_op jit(solution)/shard_map/ppermute | solution.py:284
  93.7 2.3 %collective-permute-start.1 = (bf16[128,2048]{1,0:T(8,128)(2,1)S(1)}, bf16[128,2048]{1,0:T(8,128)(2,1)S(1)}, u32[]{:S(2)}, u32[]{:S(2)}) collective-permute-start(bf16[128,2048]{1,0:T(8,128)(2,1)S(1)} %get-tuple-element.14), channel_id=1, source_target_pairs={{0,1},{1,0},{2,3},{3,2},{4,5},{5,4},{6,7},{7,6},{8,9},{9,8},{10,11... | collective-permute-start | bytes 1572872 | tf_op jit(solution)/shard_map/ppermute | solution.py:284

commit v6 on v5

--- a/solution.py
+++ b/solution.py
@@ -66,7 +66,7 @@
 
 
 def pack_kernel(
-    route_hbm, qk_hbm, v_hbm, g_hbm, o_ref, upper_ref, partner_ref, route_buf, *scratch
+    route_hbm, qk_hbm, v_hbm, g_hbm, o_ref, upper_ref, partner_smem, route_buf, partner_buf, *scratch
 ):
     buffers, sems = scratch[:3], scratch[3]
     inputs = (qk_hbm, v_hbm, g_hbm)
@@ -99,7 +99,9 @@
     diagonal = grid_of(0) == grid_of(1)
     column = jnp.sum(jnp.where(diagonal, labels, 0), axis=1, keepdims=True)
     same = (labels == column) & jnp.logical_not(diagonal)
-    partner_ref[...] = jnp.sum(jnp.where(same, grid_of(0), 0), axis=0, keepdims=True)
+    partner_buf[...] = jnp.sum(jnp.where(same, grid_of(0), 0), axis=0, keepdims=True)
+    partner_store = pltpu.make_async_copy(partner_buf, partner_smem, sems.at[STEPS, 1])
+    partner_store.start()
     at_most = grid_of(0) <= grid_of(1)
 
     def head(j):
@@ -126,23 +128,26 @@
         for load in loads(step):
             load.wait()
         in_step([head(step * STEP_HEADS + j) for j in range(STEP_HEADS)])
+    partner_store.wait()
 
 
 def pack(route, qk, value, grad):
     shape = (HEADS, SLICES, MSG, 2, HEAD_DIM)
     buffer = pltpu.VMEM((TILE, HEADS * HEAD_DIM), BF16)
     hbm = pl.BlockSpec(memory_space=pltpu.HBM)
+    whole = pl.BlockSpec(memory_space=pltpu.VMEM)
     return pl.pallas_call(
         pack_kernel,
         out_shape=(
             jax.ShapeDtypeStruct(shape, BF16),
             jax.ShapeDtypeStruct((HEADS, 1), jnp.int32),
-            jax.ShapeDtypeStruct((1, TILES), jnp.int32),
+            pltpu.SMEM((1, TILES), jnp.int32),
         ),
         in_specs=[hbm, hbm, hbm, hbm],
-        out_specs=(pl.BlockSpec(memory_space=pltpu.VMEM),) * 3,
+        out_specs=(whole, whole, pl.BlockSpec(memory_space=pltpu.SMEM)),
         scratch_shapes=[
             pltpu.VMEM((HEADS, TILES), jnp.int32),
+            pltpu.VMEM((1, TILES), jnp.int32),
             buffer,
             buffer,
             buffer,
@@ -170,7 +175,7 @@
         out_specs=whole,
         compiler_params=pltpu.CompilerParams(vmem_limit_bytes=VMEM_LIMIT),
         name="swap",
-    )(partner, x)
+    )(pltpu.with_memory_space_constraint(partner, pltpu.SMEM), x)
 
 
 def finish_kernel(upper_ref, qk_ref, v_ref, g_ref, z_ref, out_ref, dqk_ref, dv_ref):

time: 97 us -> 96.5 us (level)
  no operation moved by 1% of the time
where the time goes in v6:
time: 96.5 us; the launch traced here: 96.3 us
  blocking collectives  81.5 us (84%)
  Pallas kernels  8.53 us (9%)
  starting transfers between devices  4.89 us (5%)
    all_to_all x2, blocking collectives, exchange(): return lax.all_to_all(x, 'seq', split_axis=0, concat_axis=0, tiled=True)  81.5 us
    ppermute x2, starting transfers between devices, local(): grad_qk, grad_v = lax.ppermute((grad_qk, grad_v), 'pipe', [(0, 1), (1, 0)])  4.89 us
    pallas_call x1, Pallas kernels, finish(): pl.pallas_call(finish_kernel, out_shape=(shape, shape, shape), in_specs=[...  3.26 us
    pallas_call x1, Pallas kernels, pack(): pl.pallas_call(pack_kernel, out_shape=(jax.ShapeDtypeStruct(shape, BF16),...  2.68 us
    pallas_call x3, Pallas kernels, deliver(): pl.pallas_call(deliver_kernel, out_shape=pltpu.HBM(x.shape, x.dtype), in_...  2.4 us
  transfers between devices with their start and end apart: 2, of which 1 were waited for; matrix products, arithmetic and copies ran while one was open for 0% of the time, Pallas kernels for 2%

profile of v6, /device:TPU:1, one launch (start us, length us, event | category | flops | bytes accessed | tf_op | source)
XLA Modules:
  0.0 96.3 jit_solution(5371626708444302724)
XLA Ops:
  0.6 2.7 %pack.1 = (bf16[16,8,17,2,128]{4,3,2,1,0:T(2,128)(2,1)S(1)}, s32[16,1]{1,0:T(8,128)S(1)}, s32[1,128]{1,0:T(1,128)S(4)}) custom-call(s32[16,128]{1,0:T(8,128)} %bitcast.22, bf16[128,2048]{1,0:T(8,128)(2,1)} %bitcast.12, bf16[128,2048]{1,0:T(8,128)(2,1)} %bitcast.14, bf16[128,2048]{1,0:T(8,128)(2,1)} %bitcast.16), custom_call_target="tpu_custom_call" | custom-call | tf_op jit(solution)/shard_map/pack/pallas_call | solution.py:139
  3.3 44.7 %all_to_all.10.x_ref = bf16[128,17,2,128]{3,2,1,0:T(2,128)(2,1)S(1)} all-to-all(bf16[128,17,2,128]{3,2,1,0:T(2,128)(2,1)S(1)} %bitcast.18), channel_id=1, replica_groups=mesh['seq'=128,'pipe'=2] {'seq'}, dimensions={0} | all-to-all | bytes 2228224 | tf_op jit(solution)/shard_map/all_to_all | solution.py:279
  48.0 0.2 swap.1
  48.2 0.0 copy-start
  48.2 0.0 copy-start.1
  48.2 0.0 copy-start.2
  48.2 36.8 %all_to_all.11 = bf16[128,17,2,128]{3,2,1,0:T(2,128)(2,1)S(1)} all-to-all(bf16[128,17,2,128]{3,2,1,0:T(2,128)(2,1)S(1)} %swap.1), channel_id=1, replica_groups=mesh['seq'=128,'pipe'=2] {'seq'}, dimensions={0} | all-to-all | bytes 2228224 | tf_op jit(solution)/shard_map/all_to_all | solution.py:279
  85.0 0.0 copy-done
  85.1 0.0 copy-done.1
  85.1 0.0 copy-done.2
  85.1 3.3 %finish.1 = (bf16[128,2048]{1,0:T(8,128)(2,1)S(1)}, bf16[128,2048]{1,0:T(8,128)(2,1)S(1)}, bf16[128,2048]{1,0:T(8,128)(2,1)S(1)}) custom-call(s32[16,1]{1,0:T(8,128)S(1)} %get-tuple-element.9.upper_ref, bf16[128,2048]{1,0:T(8,128)(2,1)S(1)} %bitcast.13, bf16[128,2048]{1,0:T(8,128)(2,1)S(1)} %bitcast.15, bf16[128,2048]{1,0:T(8,128)(2,1)S(1)} %bitcast.17, ...), custom_call_target="tpu_custom_call" | custom-call | tf_op jit(solution)/shard_map/finish/pallas_call | solution.py:247
  88.3 4.8 %collective-permute-start = (bf16[128,2048]{1,0:T(8,128)(2,1)S(1)}, bf16[128,2048]{1,0:T(8,128)(2,1)S(1)}, u32[]{:S(2)}, u32[]{:S(2)}) collective-permute-start(bf16[128,2048]{1,0:T(8,128)(2,1)S(1)} %get-tuple-element.13), channel_id=1, source_target_pairs={{0,1},{1,0},{2,3},{3,2},{4,5},{5,4},{6,7},{7,6},{8,9},{9,8},{10,11... | collective-permute-start | bytes 1572872 | tf_op jit(solution)/shard_map/ppermute | solution.py:289
  93.1 0.1 collective-permute-start.1
  93.2 0.8 deliver.3
  94.0 0.6 collective-permute-done.x_ref
  94.7 0.8 deliver.4
  95.5 0.0 collective-permute-done.1.x_ref
  95.5 0.8 deliver.5
Async XLA Ops:
  48.2 36.9 %copy-start = (bf16[1,128,2048]{2,1,0:T(8,128)(2,1)S(1)}, bf16[1,128,2048]{2,1,0:T(8,128)(2,1)}, u32[]{:S(2)}) copy-start(bf16[1,128,2048]{2,1,0:T(8,128)(2,1)} %param.4) | copy-start | bytes 1572868
  48.2 36.9 %copy-start.1 = (bf16[1,128,2048]{2,1,0:T(8,128)(2,1)S(1)}, bf16[1,128,2048]{2,1,0:T(8,128)(2,1)}, u32[]{:S(2)}) copy-start(bf16[1,128,2048]{2,1,0:T(8,128)(2,1)} %param.5) | copy-start | bytes 1572868
  48.2 36.9 %copy-start.2 = (bf16[1,128,2048]{2,1,0:T(8,128)(2,1)S(1)}, bf16[1,128,2048]{2,1,0:T(8,128)(2,1)}, u32[]{:S(2)}) copy-start(bf16[1,128,2048]{2,1,0:T(8,128)(2,1)} %param.6) | copy-start | bytes 1572868
  88.3 6.3 %collective-permute-start = (bf16[128,2048]{1,0:T(8,128)(2,1)S(1)}, bf16[128,2048]{1,0:T(8,128)(2,1)S(1)}, u32[]{:S(2)}, u32[]{:S(2)}) collective-permute-start(bf16[128,2048]{1,0:T(8,128)(2,1)S(1)} %get-tuple-element.13), channel_id=1, source_target_pairs={{0,1},{1,0},{2,3},{3,2},{4,5},{5,4},{6,7},{7,6},{8,9},{9,8},{10,11... | collective-permute-start | bytes 1572872 | tf_op jit(solution)/shard_map/ppermute | solution.py:289
  93.1 2.3 %collective-permute-start.1 = (bf16[128,2048]{1,0:T(8,128)(2,1)S(1)}, bf16[128,2048]{1,0:T(8,128)(2,1)S(1)}, u32[]{:S(2)}, u32[]{:S(2)}) collective-permute-start(bf16[128,2048]{1,0:T(8,128)(2,1)S(1)} %get-tuple-element.14), channel_id=1, source_target_pairs={{0,1},{1,0},{2,3},{3,2},{4,5},{5,4},{6,7},{7,6},{8,9},{9,8},{10,11... | collective-permute-start | bytes 1572872 | tf_op jit(solution)/shard_map/ppermute | solution.py:289

commit v7 on v6

--- a/solution.py
+++ b/solution.py
@@ -14,7 +14,7 @@
 SLICES = 8
 PAIRS = TILE // SLICES // 2
 MSG = 2 * PAIRS + 1
-STEP_HEADS = 8
+STEP_HEADS = 16
 STEPS = HEADS // STEP_HEADS
 STEP_COLS = STEP_HEADS * HEAD_DIM
 EPSILON = 1e-06
@@ -106,13 +106,13 @@
 
     def head(j):
         upper = uppers[j : j + 1, :] > 0.0
+        _, normed = normalise(qk_buf[:, head_columns(j)].astype(F32))
+        o_ref[j, :, 0:PAIRS] = normed.reshape(SLICES, PAIRS, 2, HEAD_DIM)
+        yield
         value = v_buf[:, head_columns(j)]
         grad = g_buf[:, head_columns(j)]
-        _, normed = normalise(qk_buf[:, head_columns(j)].astype(F32))
         second = pick(upper, grad, value)
-        o_ref[j, :, 0:PAIRS] = normed.reshape(SLICES, PAIRS, 2, HEAD_DIM)
         o_ref[j, :, PAIRS : 2 * PAIRS] = second.reshape(SLICES, PAIRS, 2, HEAD_DIM)
-        yield
         weights = jnp.where(at_most, jnp.exp2(dot_nt(normed, normed) * SCALE_LOG2), 0.0)
         grad_probs = dot_nt(value, grad)
         yield
@@ -125,9 +125,14 @@
         o_ref[j, :, 2 * PAIRS] = stats.reshape(SLICES, 2, TILE)
 
     for step in range(STEPS):
-        for load in loads(step):
+        qk_load, *other_loads = loads(step)
+        qk_load.wait()
+        heads_here = [head(step * STEP_HEADS + j) for j in range(STEP_HEADS)]
+        for one in heads_here:
+            next(one)
+        for load in other_loads:
             load.wait()
-        in_step([head(step * STEP_HEADS + j) for j in range(STEP_HEADS)])
+        in_step(heads_here)
     partner_store.wait()
 
 

time: 96.5 us -> 96.4 us (level)
  no operation moved by 1% of the time
where the time goes in v7:
time: 96.4 us; the launch traced here: 96.2 us
  blocking collectives  81.5 us (85%)
  Pallas kernels  8.42 us (9%)
  starting transfers between devices  4.89 us (5%)
    all_to_all x2, blocking collectives, exchange(): return lax.all_to_all(x, 'seq', split_axis=0, concat_axis=0, tiled=True)  81.5 us
    ppermute x2, starting transfers between devices, local(): grad_qk, grad_v = lax.ppermute((grad_qk, grad_v), 'pipe', [(0, 1), (1, 0)])  4.89 us
    pallas_call x1, Pallas kernels, finish(): pl.pallas_call(finish_kernel, out_shape=(shape, shape, shape), in_specs=[...  3.26 us
    pallas_call x1, Pallas kernels, pack(): pl.pallas_call(pack_kernel, out_shape=(jax.ShapeDtypeStruct(shape, BF16),...  2.57 us
    pallas_call x3, Pallas kernels, deliver(): pl.pallas_call(deliver_kernel, out_shape=pltpu.HBM(x.shape, x.dtype), in_...  2.4 us
  transfers between devices with their start and end apart: 2, of which 1 were waited for; matrix products, arithmetic and copies ran while one was open for 0% of the time, Pallas kernels for 2%

profile of v7, /device:TPU:1, one launch (start us, length us, event | category | flops | bytes accessed | tf_op | source)
XLA Modules:
  0.0 96.2 jit_solution(1287927408999340727)
XLA Ops:
  0.6 2.6 %pack.1 = (bf16[16,8,17,2,128]{4,3,2,1,0:T(2,128)(2,1)S(1)}, s32[16,1]{1,0:T(8,128)S(1)}, s32[1,128]{1,0:T(1,128)S(4)}) custom-call(s32[16,128]{1,0:T(8,128)} %bitcast.22, bf16[128,2048]{1,0:T(8,128)(2,1)} %bitcast.12, bf16[128,2048]{1,0:T(8,128)(2,1)} %bitcast.14, bf16[128,2048]{1,0:T(8,128)(2,1)} %bitcast.16), custom_call_target="tpu_custom_call" | custom-call | tf_op jit(solution)/shard_map/pack/pallas_call | solution.py:144
  3.2 44.7 %all_to_all.10.x_ref = bf16[128,17,2,128]{3,2,1,0:T(2,128)(2,1)S(1)} all-to-all(bf16[128,17,2,128]{3,2,1,0:T(2,128)(2,1)S(1)} %bitcast.18), channel_id=1, replica_groups=mesh['seq'=128,'pipe'=2] {'seq'}, dimensions={0} | all-to-all | bytes 2228224 | tf_op jit(solution)/shard_map/all_to_all | solution.py:284
  47.9 0.2 swap.1
  48.1 0.0 copy-start
  48.1 0.0 copy-start.1
  48.1 0.0 copy-start.2
  48.1 36.8 %all_to_all.11 = bf16[128,17,2,128]{3,2,1,0:T(2,128)(2,1)S(1)} all-to-all(bf16[128,17,2,128]{3,2,1,0:T(2,128)(2,1)S(1)} %swap.1), channel_id=1, replica_groups=mesh['seq'=128,'pipe'=2] {'seq'}, dimensions={0} | all-to-all | bytes 2228224 | tf_op jit(solution)/shard_map/all_to_all | solution.py:284
  84.9 0.0 copy-done
  84.9 0.0 copy-done.1
  84.9 0.0 copy-done.2
  85.0 3.3 %finish.1 = (bf16[128,2048]{1,0:T(8,128)(2,1)S(1)}, bf16[128,2048]{1,0:T(8,128)(2,1)S(1)}, bf16[128,2048]{1,0:T(8,128)(2,1)S(1)}) custom-call(s32[16,1]{1,0:T(8,128)S(1)} %get-tuple-element.9.upper_ref, bf16[128,2048]{1,0:T(8,128)(2,1)S(1)} %bitcast.13, bf16[128,2048]{1,0:T(8,128)(2,1)S(1)} %bitcast.15, bf16[128,2048]{1,0:T(8,128)(2,1)S(1)} %bitcast.17, ...), custom_call_target="tpu_custom_call" | custom-call | tf_op jit(solution)/shard_map/finish/pallas_call | solution.py:252
  88.2 4.8 %collective-permute-start = (bf16[128,2048]{1,0:T(8,128)(2,1)S(1)}, bf16[128,2048]{1,0:T(8,128)(2,1)S(1)}, u32[]{:S(2)}, u32[]{:S(2)}) collective-permute-start(bf16[128,2048]{1,0:T(8,128)(2,1)S(1)} %get-tuple-element.13), channel_id=1, source_target_pairs={{0,1},{1,0},{2,3},{3,2},{4,5},{5,4},{6,7},{7,6},{8,9},{9,8},{10,11... | collective-permute-start | bytes 1572872 | tf_op jit(solution)/shard_map/ppermute | solution.py:294
  93.0 0.1 collective-permute-start.1
  93.1 0.8 deliver.3
  93.9 0.6 collective-permute-done.x_ref
  94.5 0.8 deliver.4
  95.4 0.0 collective-permute-done.1.x_ref
  95.4 0.8 deliver.5
Async XLA Ops:
  48.1 36.9 %copy-start = (bf16[1,128,2048]{2,1,0:T(8,128)(2,1)S(1)}, bf16[1,128,2048]{2,1,0:T(8,128)(2,1)}, u32[]{:S(2)}) copy-start(bf16[1,128,2048]{2,1,0:T(8,128)(2,1)} %param.4) | copy-start | bytes 1572868
  48.1 36.9 %copy-start.1 = (bf16[1,128,2048]{2,1,0:T(8,128)(2,1)S(1)}, bf16[1,128,2048]{2,1,0:T(8,128)(2,1)}, u32[]{:S(2)}) copy-start(bf16[1,128,2048]{2,1,0:T(8,128)(2,1)} %param.5) | copy-start | bytes 1572868
  48.1 36.9 %copy-start.2 = (bf16[1,128,2048]{2,1,0:T(8,128)(2,1)S(1)}, bf16[1,128,2048]{2,1,0:T(8,128)(2,1)}, u32[]{:S(2)}) copy-start(bf16[1,128,2048]{2,1,0:T(8,128)(2,1)} %param.6) | copy-start | bytes 1572868
  88.2 6.3 %collective-permute-start = (bf16[128,2048]{1,0:T(8,128)(2,1)S(1)}, bf16[128,2048]{1,0:T(8,128)(2,1)S(1)}, u32[]{:S(2)}, u32[]{:S(2)}) collective-permute-start(bf16[128,2048]{1,0:T(8,128)(2,1)S(1)} %get-tuple-element.13), channel_id=1, source_target_pairs={{0,1},{1,0},{2,3},{3,2},{4,5},{5,4},{6,7},{7,6},{8,9},{9,8},{10,11... | collective-permute-start | bytes 1572872 | tf_op jit(solution)/shard_map/ppermute | solution.py:294
  93.0 2.3 %collective-permute-start.1 = (bf16[128,2048]{1,0:T(8,128)(2,1)S(1)}, bf16[128,2048]{1,0:T(8,128)(2,1)S(1)}, u32[]{:S(2)}, u32[]{:S(2)}) collective-permute-start(bf16[128,2048]{1,0:T(8,128)(2,1)S(1)} %get-tuple-element.14), channel_id=1, source_target_pairs={{0,1},{1,0},{2,3},{3,2},{4,5},{5,4},{6,7},{7,6},{8,9},{9,8},{10,11... | collective-permute-start | bytes 1572872 | tf_op jit(solution)/shard_map/ppermute | solution.py:294

commit v8 on v7

--- a/solution.py
+++ b/solution.py
@@ -183,7 +183,7 @@
     )(pltpu.with_memory_space_constraint(partner, pltpu.SMEM), x)
 
 
-def finish_kernel(upper_ref, qk_ref, v_ref, g_ref, z_ref, out_ref, dqk_ref, dv_ref):
+def finish_kernel(upper_ref, qk_ref, v_ref, g_ref, z_ref, out_ref, grads_ref):
     uppers = upper_ref[...]
     ahead = grid_of(0) - grid_of(1)
 
@@ -236,11 +236,11 @@
         grad_normed = dot_nn(scores, keys) + dot_tn(own_s, normed)
         yield
         out_ref[:, head_columns(j)] = jnp.where(upper, along, across).astype(BF16)
-        dv_ref[:, head_columns(j)] = jnp.where(upper, across, along).astype(BF16)
+        grads_ref[1, :, head_columns(j)] = jnp.where(upper, across, along).astype(BF16)
         grad_normed = (grad_normed * SCALE).astype(BF16).astype(F32)
         inner = jnp.mean(raw * grad_normed, axis=-1, keepdims=True)
         grad_input = factor * grad_normed - raw * (factor**3 * inner)
-        dqk_ref[:, head_columns(j)] = grad_input.astype(BF16)
+        grads_ref[0, :, head_columns(j)] = grad_input.astype(BF16)
 
     for start in range(0, HEADS, GROUP):
         in_step([head(start + j) for j in range(GROUP)])
@@ -251,9 +251,9 @@
     whole = pl.BlockSpec(memory_space=pltpu.VMEM)
     return pl.pallas_call(
         finish_kernel,
-        out_shape=(shape, shape, shape),
+        out_shape=(shape, jax.ShapeDtypeStruct((2, *shape.shape), shape.dtype)),
         in_specs=[whole] * 5,
-        out_specs=(whole, whole, whole),
+        out_specs=(whole, whole),
         compiler_params=pltpu.CompilerParams(vmem_limit_bytes=VMEM_LIMIT),
         name="finish",
     )(upper, qk, value, grad, z)
@@ -277,6 +277,30 @@
             flops=0, bytes_accessed=2 * x.size * x.dtype.itemsize, transcendentals=0
         ),
         name="deliver",
+    )(x)
+
+
+def deliver_pair_kernel(x_ref, a_hbm, b_hbm, sems):
+    copies = [
+        pltpu.make_async_copy(x_ref.at[i], o_hbm, sems.at[i])
+        for i, o_hbm in enumerate((a_hbm, b_hbm))
+    ]
+    for copy in copies:
+        copy.start()
+    for copy in copies:
+        copy.wait()
+
+
+def deliver_pair(x):
+    hbm = pl.BlockSpec(memory_space=pltpu.HBM)
+    return pl.pallas_call(
+        deliver_pair_kernel,
+        out_shape=(pltpu.HBM(x.shape[1:], x.dtype),) * 2,
+        in_specs=[pl.BlockSpec(memory_space=pltpu.VMEM)],
+        out_specs=(hbm, hbm),
+        scratch_shapes=[pltpu.SemaphoreType.DMA((2,))],
+        compiler_params=pltpu.CompilerParams(vmem_limit_bytes=VMEM_LIMIT),
+        name="deliver_pair",
     )(x)
 
 
@@ -290,9 +314,9 @@
     packed, upper, partner = pack(route.T, *rows)
     slices = exchange(packed.reshape(TILES, MSG, 2, HEAD_DIM))
     theirs = exchange(swap(partner, slices)).reshape(HEADS, SLICES, MSG, 2, HEAD_DIM)
-    out, grad_qk, grad_v = finish(upper, *rows, theirs)
-    grad_qk, grad_v = lax.ppermute((grad_qk, grad_v), "pipe", [(0, 1), (1, 0)])
-    out, grad_qk, grad_v = deliver(out), deliver(grad_qk), deliver(grad_v)
+    out, grads = finish(upper, *rows, theirs)
+    grads = lax.ppermute(grads, "pipe", [(0, 1), (1, 0)])
+    out, (grad_qk, grad_v) = deliver(out), deliver_pair(grads)
     return (out[None], grad_qk[None], grad_v[None])
 
 

time: 96.4 us -> 96.5 us (level)
    pallas_call x3 -> x1, Pallas kernels: 2.4 us -> 0.8 us  [deliver(): pl.pallas_call(deliver_kernel, out_shape=pltpu.HBM(x.shape, x.dtype), in_...]
    pallas_call x1 -> x2, Pallas kernels: 3.26 us -> 4.24 us  [the longest x1 3.26 us: finish(): pl.pallas_call(finish_kernel, out_shape=(shape, jax.ShapeDtypeStruct((2,...]
    ppermute x2 -> x1, starting transfers between devices: 4.89 us -> 4.79 us  [local(): grads = lax.ppermute(grads, 'pipe', [(0, 1), (1, 0)])]
  transfers between devices with their start and end apart: 2 -> 1, of which waited for: 1 -> 1; matrix products, arithmetic and copies ran while one was open for 0% -> 0% of each run, Pallas kernels for 2% -> 1%
where the time goes in v8:
time: 96.5 us; the launch traced here: 96.3 us
  blocking collectives  81.5 us (84%)
  Pallas kernels  7.79 us (8%)
  starting transfers between devices  4.79 us (5%)
  waiting for transfers between devices  1.48 us (2%)
    all_to_all x2, blocking collectives, exchange(): return lax.all_to_all(x, 'seq', split_axis=0, concat_axis=0, tiled=True)  81.5 us
    ppermute x1, starting transfers between devices, local(): grads = lax.ppermute(grads, 'pipe', [(0, 1), (1, 0)])  4.79 us
    pallas_call x1, Pallas kernels, finish(): pl.pallas_call(finish_kernel, out_shape=(shape, jax.ShapeDtypeStruct((2,...  3.26 us
    pallas_call x1, Pallas kernels, pack(): pl.pallas_call(pack_kernel, out_shape=(jax.ShapeDtypeStruct(shape, BF16),...  2.57 us
  transfers between devices with their start and end apart: 1, of which 1 were waited for; matrix products, arithmetic and copies ran while one was open for 0% of the time, Pallas kernels for 1%

profile of v8, /device:TPU:1, one launch (start us, length us, event | category | flops | bytes accessed | tf_op | source)
XLA Modules:
  0.0 96.3 jit_solution(14038456276449352773)
XLA Ops:
  0.6 2.6 %pack.1 = (bf16[16,8,17,2,128]{4,3,2,1,0:T(2,128)(2,1)S(1)}, s32[16,1]{1,0:T(8,128)S(1)}, s32[1,128]{1,0:T(1,128)S(4)}) custom-call(s32[16,128]{1,0:T(8,128)} %bitcast.20, bf16[128,2048]{1,0:T(8,128)(2,1)} %bitcast.12, bf16[128,2048]{1,0:T(8,128)(2,1)} %bitcast.14, bf16[128,2048]{1,0:T(8,128)(2,1)} %bitcast.16), custom_call_target="tpu_custom_call" | custom-call | tf_op jit(solution)/shard_map/pack/pallas_call | solution.py:144
  3.2 44.7 %all_to_all.10.x_ref = bf16[128,17,2,128]{3,2,1,0:T(2,128)(2,1)S(1)} all-to-all(bf16[128,17,2,128]{3,2,1,0:T(2,128)(2,1)S(1)} %bitcast.18), channel_id=1, replica_groups=mesh['seq'=128,'pipe'=2] {'seq'}, dimensions={0} | all-to-all | bytes 2228224 | tf_op jit(solution)/shard_map/all_to_all | solution.py:308
  47.9 0.2 swap.1
  48.1 0.0 copy-start
  48.1 0.0 copy-start.1
  48.1 0.0 copy-start.2
  48.1 36.8 %all_to_all.11 = bf16[128,17,2,128]{3,2,1,0:T(2,128)(2,1)S(1)} all-to-all(bf16[128,17,2,128]{3,2,1,0:T(2,128)(2,1)S(1)} %swap.1), channel_id=1, replica_groups=mesh['seq'=128,'pipe'=2] {'seq'}, dimensions={0} | all-to-all | bytes 2228224 | tf_op jit(solution)/shard_map/all_to_all | solution.py:308
  84.9 0.0 copy-done
  84.9 0.0 copy-done.1
  84.9 0.0 copy-done.2
  85.0 3.3 %finish.1 = (bf16[128,2048]{1,0:T(8,128)(2,1)S(1)}, bf16[2,128,2048]{2,1,0:T(8,128)(2,1)S(1)}) custom-call(s32[16,1]{1,0:T(8,128)S(1)} %get-tuple-element.10.upper_ref, bf16[128,2048]{1,0:T(8,128)(2,1)S(1)} %bitcast.13, bf16[128,2048]{1,0:T(8,128)(2,1)S(1)} %bitcast.15, bf16[128,2048]{1,0:T(8,128)(2,1)S(1)} %bitcast.17, bf16[16,8,17,2,128]{4,3,2,1,0:T(2,128)(2,1)S(1)} %bitcast.11), custom_call_target="tpu_custom_call" | custom-call | tf_op jit(solution)/shard_map/finish/pallas_call | solution.py:252
  88.2 4.8 %collective-permute-start = (bf16[2,128,2048]{2,1,0:T(8,128)(2,1)S(1)}, bf16[2,128,2048]{2,1,0:T(8,128)(2,1)S(1)}, u32[]{:S(2)}, u32[]{:S(2)}) collective-permute-start(bf16[2,128,2048]{2,1,0:T(8,128)(2,1)S(1)} %get-tuple-element.14), channel_id=1, source_target_pairs={{0,1},{1,0},{2,3},{3,2},{4,5},{5,4},{6,7},{7,6},{8,9},{9,8},{10,11... | collective-permute-start | bytes 3145736 | tf_op jit(solution)/shard_map/ppermute | solution.py:318
  93.0 0.8 deliver.1
  93.8 1.5 %collective-permute-done.x_ref = bf16[2,128,2048]{2,1,0:T(8,128)(2,1)S(1)} collective-permute-done((bf16[2,128,2048]{2,1,0:T(8,128)(2,1)S(1)}, bf16[2,128,2048]{2,1,0:T(8,128)(2,1)S(1)}, u32[]{:S(2)}, u32[]{:S(2)}) %collective-permute-start) | collective-permute-done | bytes 1048608 | tf_op jit(solution)/shard_map/ppermute | solution.py:318
  95.3 1.0 %deliver_pair.1 = (bf16[128,2048]{1,0:T(8,128)(2,1)}, bf16[128,2048]{1,0:T(8,128)(2,1)}) custom-call(bf16[2,128,2048]{2,1,0:T(8,128)(2,1)S(1)} %collective-permute-done.x_ref), custom_call_target="tpu_custom_call" | custom-call | tf_op jit(solution)/shard_map/deliver_pair/pallas_call | solution.py:296
Async XLA Ops:
  48.1 36.9 %copy-start = (bf16[1,128,2048]{2,1,0:T(8,128)(2,1)S(1)}, bf16[1,128,2048]{2,1,0:T(8,128)(2,1)}, u32[]{:S(2)}) copy-start(bf16[1,128,2048]{2,1,0:T(8,128)(2,1)} %param.4) | copy-start | bytes 1572868
  48.1 36.9 %copy-start.1 = (bf16[1,128,2048]{2,1,0:T(8,128)(2,1)S(1)}, bf16[1,128,2048]{2,1,0:T(8,128)(2,1)}, u32[]{:S(2)}) copy-start(bf16[1,128,2048]{2,1,0:T(8,128)(2,1)} %param.5) | copy-start | bytes 1572868
  48.1 36.9 %copy-start.2 = (bf16[1,128,2048]{2,1,0:T(8,128)(2,1)S(1)}, bf16[1,128,2048]{2,1,0:T(8,128)(2,1)}, u32[]{:S(2)}) copy-start(bf16[1,128,2048]{2,1,0:T(8,128)(2,1)} %param.6) | copy-start | bytes 1572868
  88.2 7.1 %collective-permute-start = (bf16[2,128,2048]{2,1,0:T(8,128)(2,1)S(1)}, bf16[2,128,2048]{2,1,0:T(8,128)(2,1)S(1)}, u32[]{:S(2)}, u32[]{:S(2)}) collective-permute-start(bf16[2,128,2048]{2,1,0:T(8,128)(2,1)S(1)} %get-tuple-element.14), channel_id=1, source_target_pairs={{0,1},{1,0},{2,3},{3,2},{4,5},{5,4},{6,7},{7,6},{8,9},{9,8},{10,11... | collective-permute-start | bytes 3145736 | tf_op jit(solution)/shard_map/ppermute | solution.py:318
